TPU v7x, 256 devices: a whole 4x4x8 slice. The times are simulated.
256 devices in a mesh: occ: 128 (over z, y, x), aux: 2 (over core).
Axes of the slice: x: 4, y: 4, z: 8, core: 2. Of those that a mesh axis runs over, the one named last changes fastest.
Arguments:
- three_index: bfloat16 [2, 256, 1280, 1152], P('aux', None, 'occ'), may hold values from -0.8984375 to 0.8984375
- partners: int32 [256], replicated, may hold values from 0 to 255, each once
- vir_blocks: int32 [512, 2, 8], replicated, may hold values from 0 to 8, as said below
- fit_blocks: int32 [512, 2, 2, 8], P('occ', None, 'aux'), may hold values from 0 to 9, as said below
- block_counts: int32 [512, 2], P('occ'), may hold values from 1 to 8
- virt_energies: float32 [512, 1024], P('occ'), may hold values from 0.1 to 1.5
- occ_energies: float32 [256], replicated, may hold values from -1 to -0.25
Outputs:
- amplitudes: bfloat16 [512, 1024, 1024], P('occ', 'aux')
Inputs may be any that keep to these rules, and one draw needn't show every extreme that they name: `vir_blocks`: each pair's 8 positions for one side are distinct. `fit_blocks`: each pair's 8 positions for one side and half are distinct.
All inputs are finite; a program needn't handle non-finite values.
Results may differ from a plain program's by a relative error of at most 0.001.
Values may be sent and summed in bfloat16 or wider, within the bound.
No kernel may reach another device: no remote copies, remote signals or barrier semaphores. Data moves between devices by JAX's collectives and lax.ppermute only.
A program may use at most 192 MiB of HBM per device.

v0:
```python
import jax
import jax.numpy as jnp
from jax import lax
from jax.sharding import PartitionSpec as P

BLK = 128
OCC_DEV = 2
PARTNERS = 2
VB = 8
FB = 8


def select_blocks(matrix, fit_pos, vir_pos):
    blocked = matrix.reshape(matrix.shape[0] // BLK, BLK, matrix.shape[1] // BLK, BLK)
    chosen = blocked[fit_pos][:, :, vir_pos, :]
    return chosen.reshape(fit_pos.shape[0], BLK, vir_pos.shape[0] * BLK)


def per_device(
    three_index, partners, vir_blocks, fit_blocks, block_counts, virt_energies, occ_energies
):
    orbital_major = three_index[0]
    row_count = orbital_major.shape[1]
    owners = lax.axis_size("occ")
    owner_index = lax.axis_index("occ")
    pairs_dev = OCC_DEV * PARTNERS
    pair_width = VB * BLK
    own_rows = lax.all_to_all(orbital_major, "occ", split_axis=0, concat_axis=1, tiled=True)
    my_vir = lax.dynamic_slice_in_dim(vir_blocks, owner_index * pairs_dev, pairs_dev, 0)
    my_partners = lax.dynamic_slice_in_dim(partners, owner_index * PARTNERS, PARTNERS, 0)
    partner_ids = jnp.broadcast_to(
        partners.reshape(owners, 1, PARTNERS), (owners, OCC_DEV, PARTNERS)
    ).reshape(-1)
    blocked = orbital_major.reshape(
        orbital_major.shape[0], row_count, orbital_major.shape[2] // BLK, BLK
    )
    partner_slabs = jnp.take(blocked, partner_ids, axis=0)
    block_pick = vir_blocks[:, 1, :][:, None, :, None]
    outgoing = jnp.take_along_axis(partner_slabs, block_pick, axis=2)
    outgoing = outgoing.reshape(partner_ids.shape[0], row_count, pair_width)
    arrived = lax.all_to_all(outgoing, "occ", split_axis=0, concat_axis=1, tiled=True)
    coulomb_terms = []
    for p in range(pairs_dev):
        k = p // PARTNERS
        fit_pos = fit_blocks[p, :, 0, :]
        left_side = select_blocks(own_rows[k], fit_pos[0], my_vir[p, 0])
        right_side = arrived[p].reshape(-1, BLK, pair_width)[fit_pos[1]]
        fit_count = block_counts[p, 1]
        live_fit = jnp.arange(FB, dtype=jnp.int32) < fit_count
        masked = jnp.where(live_fit[:, None, None], left_side, jnp.zeros((), left_side.dtype))
        coulomb = lax.dot_general(
            masked.reshape(-1, pair_width),
            right_side.reshape(-1, pair_width),
            (((0,), (0,)), ((), ())),
            preferred_element_type=jnp.float32,
        )
        coulomb_terms.append(coulomb)
    stacked = jnp.stack(coulomb_terms)
    halves = lax.psum_scatter(stacked, "aux", scatter_dimension=1, tiled=True)
    half_rows = halves.shape[1]
    row_index = lax.axis_index("aux") * half_rows + jnp.arange(half_rows, dtype=jnp.int32)
    col_index = jnp.arange(pair_width, dtype=jnp.int32)
    slots = jnp.arange(pairs_dev, dtype=jnp.int32)
    occ_left = occ_energies[owner_index * OCC_DEV + slots // PARTNERS]
    occ_right = occ_energies[my_partners[slots % PARTNERS]]
    row_energies = jnp.take(virt_energies, row_index, axis=1)
    denominator = (
        row_energies[:, :, None]
        + virt_energies[:, None, :]
        - occ_left[:, None, None]
        - occ_right[:, None, None]
    )
    live_limit = block_counts[:, 0] * BLK
    live_mask = (row_index[None, :] < live_limit[:, None])[:, :, None] & (
        col_index[None, :] < live_limit[:, None]
    )[:, None, :]
    amplitude = jnp.where(live_mask, -halves / denominator, 0.0)
    return amplitude.astype(jnp.bfloat16)


def solution(mesh):
    return jax.shard_map(
        per_device,
        mesh=mesh,
        in_specs=(
            P("aux", None, "occ", None),
            P(),
            P(),
            P("occ", None, "aux", None),
            P("occ", None),
            P("occ", None),
            P(),
        ),
        out_specs=P("occ", "aux", None),
        check_vma=False,
    )
```

profile of v0, /device:TPU:1, one launch (start us, length us, event | category | flops | bytes accessed | tf_op | source)
XLA Modules:
  0.0 794.0 jit_solution(14958505249203691625)
XLA Ops:
  6.5 10.0 %copy.65 = bf16[1,256,10,1152]{3,2,1,0:T(8,128)(2,1)} copy(bf16[1,256,10,1152]{3,1,2,0:T(8,128)(2,1)} %param.7) | data formatting | bytes 11796480 | tf_op args[0]
  16.5 17.4 %all-to-all-start = ((bf16[256,10,1152]{2,1,0:T(8,128)(2,1)}), bf16[256,10,1152]{2,1,0:T(8,128)(2,1)}, u32[]{:S(2)}, u32[]{:S(2)}) async-start(bf16[256,10,1152]{2,1,0:T(8,128)(2,1)} %bitcast.126), calls=%async_computation | async-start | bytes 18874368 | tf_op jit(solution)/shard_map/all_to_all | solution.py:28
  34.5 9.0 %copy.41 = bf16[1,256,10,1152]{1,3,2,0:T(8,128)(2,1)} copy(bf16[1,256,10,1152]{3,1,2,0:T(8,128)(2,1)} %param.7) | data formatting | bytes 11796480 | tf_op args[0]
  43.7 13.2 %copy.42 = bf16[256,10,9,128]{3,1,2,0:T(8,128)(2,1)} copy(bf16[256,10,9,128]{0,3,2,1:T(8,128)(2,1)} %bitcast.128) | data formatting | bytes 11796480 | tf_op jit(solution)/shard_map/reshape;squeeze | solution.py:34
  57.0 18.9 %gather_fusion.2 = bf16[512,10,9,128]{3,1,2,0:T(8,128)(2,1)} fusion(bf16[256,10,9,128]{3,1,2,0:T(8,128)(2,1)} %copy.42, s32[1024]{0:T(1024)S(1)} %pad_clamp_fusion.14), kind=kCustom, calls=%fused_computation.2 | custom fusion | bytes 23595008 | tf_op jit(solution)/shard_map/jit(_take)/gather | solution.py:37
  75.9 17.3 %broadcast_select_fusion = bf16[512,10,9,128]{3,1,2,0:T(8,128)(2,1)} fusion(bf16[512,10,9,128]{3,1,2,0:T(8,128)(2,1)} %gather_fusion.2, pred[512]{0:T(512)(128)(4,1)S(1)} %compare_and_fusion.2), kind=kLoop, calls=%fused_computation.18 | loop fusion | flops 5898240 | bytes 23593472 | tf_op jit(solution)/shard_map/jit(_take)/select_n | solution.py:37
  93.3 45.7 %gather_fusion.17 = bf16[4096,10,128]{2,1,0:T(8,128)(2,1)} fusion(bf16[512,10,9,128]{3,1,2,0:T(8,128)(2,1)} %broadcast_select_fusion, s32[4096]{0:T(1024)S(1)} %reshape.822), kind=kCustom, calls=%fused_computation.17 | custom fusion | bytes 21004288 | tf_op jit(solution)/shard_map/jit(take_along_axis)/gather | solution.py:39
  138.9 22.7 %copy.44 = bf16[512,8,10,128]{0,3,1,2:T(8,128)(2,1)} copy(bf16[512,8,10,128]{3,2,1,0:T(8,128)(2,1)} %bitcast.125) | data formatting | bytes 20971520 | tf_op jit(solution)/shard_map/jit(take_along_axis)/gather | solution.py:39
  161.8 10.3 %bitcast_select_fusion = bf16[512,10,1024]{0,2,1:T(8,128)(2,1)} fusion(bf16[512,8,10,128]{0,3,1,2:T(8,128)(2,1)} %copy.44, pred[512,1024]{0,1:T(8,128)(4,1)S(1)} %bitcast.133), kind=kLoop, calls=%fused_computation.20 | loop fusion | flops 5242880 | bytes 21495808 | tf_op jit(solution)/shard_map/jit(take_along_axis)/select_n | solution.py:39
  172.2 22.7 %copy.45 = bf16[512,10,1024]{2,1,0:T(8,128)(2,1)} copy(bf16[512,10,1024]{0,2,1:T(8,128)(2,1)} %bitcast_select_fusion) | data formatting | bytes 20971520 | tf_op jit(solution)/shard_map/jit(take_along_axis)/select_n | solution.py:39
  194.8 47.1 %all-to-all-done = bf16[256,10,1152]{2,1,0:T(8,128)(2,1)} async-done(((bf16[256,10,1152]{2,1,0:T(8,128)(2,1)}), bf16[256,10,1152]{2,1,0:T(8,128)(2,1)}, u32[]{:S(2)}, u32[]{:S(2)}) %all-to-all-start) | async-done | bytes 5898272 | tf_op jit(solution)/shard_map/all_to_all | solution.py:28
  241.9 9.9 %all-to-all-start.1 = ((bf16[512,10,1024]{2,1,0:T(8,128)(2,1)}), bf16[512,10,1024]{2,1,0:T(8,128)(2,1)}, u32[]{:S(2)}, u32[]{:S(2)}) async-start(bf16[512,10,1024]{2,1,0:T(8,128)(2,1)} %copy.45), calls=%async_computation.1 | async-start | bytes 33554432 | tf_op jit(solution)/shard_map/all_to_all | solution.py:41
  255.7 8.0 %copy.64 = bf16[128,2,10,1152]{3,2,0,1:T(8,128)(2,1)} copy(bf16[128,2,10,1152]{3,2,1,0:T(8,128)(2,1)} %bitcast.3) | data formatting | bytes 11796480 | tf_op jit(solution)/shard_map/all_to_all | solution.py:28
  263.7 8.1 %fusion.20 = (bf16[1,128,10,1152]{3,2,1,0:T(8,128)(2,1)}, bf16[1,128,10,1152]{3,2,1,0:T(8,128)(2,1)}) fusion(bf16[2,128,10,1152]{3,2,1,0:T(8,128)(2,1)} %bitcast.127), kind=kLoop, calls=%fused_computation.112 | loop fusion | bytes 11796480 | tf_op jit(solution)/shard_map/slice | solution.py:46
  271.8 8.6 %reshape_squeeze.23 = bf16[10,128,9,128]{3,2,1,0:T(8,128)(2,1)} reshape(bf16[1,128,10,1152]{3,2,1,0:T(8,128)(2,1)} %get-tuple-element.13) | data formatting | bytes 5898240 | tf_op jit(solution)/shard_map/reshape;squeeze | solution.py:14
  302.3 8.4 %reshape_squeeze.27 = bf16[10,128,9,128]{3,2,1,0:T(8,128)(2,1)} reshape(bf16[1,128,10,1152]{3,2,1,0:T(8,128)(2,1)} %get-tuple-element.14) | data formatting | bytes 5898240 | tf_op jit(solution)/shard_map/reshape;squeeze | solution.py:14
  341.4 289.1 %all-to-all-done.1 = bf16[512,10,1024]{2,1,0:T(8,128)(2,1)} async-done(((bf16[512,10,1024]{2,1,0:T(8,128)(2,1)}), bf16[512,10,1024]{2,1,0:T(8,128)(2,1)}, u32[]{:S(2)}, u32[]{:S(2)}) %all-to-all-start.1) | async-done | bytes 10485792 | tf_op jit(solution)/shard_map/all_to_all | solution.py:41
  630.6 12.8 %copy.63 = bf16[128,4,10,1024]{3,1,0,2:T(4,128)(2,1)S(1)} copy(bf16[128,4,10,1024]{3,2,1,0:T(8,128)(2,1)} %bitcast.18) | data formatting | bytes 20971520 | tf_op jit(solution)/shard_map/all_to_all | solution.py:41
  643.4 18.0 %fusion.19 = (bf16[1,128,10,1024]{3,0,1,2:T(2,128)(2,1)S(1)}, bf16[1,128,10,1024]{3,0,1,2:T(2,128)(2,1)}, bf16[1,128,10,1024]{3,0,1,2:T(2,128)(2,1)}, bf16[1,128,10,1024]{3,0,1,2:T(2,128)(2,1)}) fusion(bf16[4,128,10,1024]{3,0,1,2:T(4,128)(2,1)S(1)} %bitcast.124), kind=kLoop, calls=%fused_computation.111 | loop fusion | bytes 20971520 | tf_op jit(solution)/shard_map/slice | solution.py:47
  661.4 4.9 copy.47
  666.2 6.1 reshape_squeeze.25
  672.4 7.4 copy.56
  679.7 6.1 reshape_squeeze.29
  685.9 7.4 copy.53
  693.2 6.4 reshape_squeeze.28
  699.6 7.4 copy.50
  715.5 6.5 convolution_bitcast_fusion.3
  725.8 6.6 convolution_bitcast_fusion
  736.2 6.5 convolution_bitcast_fusion.1
  750.7 6.0 pad_maximum_fusion
  761.2 19.3 %reduce-scatter.2.cloned.1.call-done = f32[4,512,1024]{2,1,0:T(8,128)} async-done(((f32[4,1024,1024]{2,1,0:T(8,128)}), f32[4,512,1024]{2,1,0:T(8,128)}) %reduce-scatter.2.cloned.1.call-update) | async-done | bytes 8388624 | tf_op jit(solution)/shard_map/reduce_scatter | solution.py:59
  780.4 6.3 select_convert_fusion
  (111 shorter events, 85.7 us)
Async XLA Ops:
  6.5 751.6 %copy-start = (f32[256]{0:T(256)S(1)}, f32[256]{0:T(256)}, u32[]{:S(2)}) copy-start(f32[256]{0:T(256)} %param.13) | copy-start | bytes 3076
  16.5 17.4 %copy-start.14 = (s32[256]{0:T(256)S(1)}, s32[256]{0:T(256)}, u32[]{:S(2)}) copy-start(s32[256]{0:T(256)} %param.8) | copy-start | bytes 3076
  16.5 225.4 %all-to-all-start = ((bf16[256,10,1152]{2,1,0:T(8,128)(2,1)}), bf16[256,10,1152]{2,1,0:T(8,128)(2,1)}, u32[]{:S(2)}, u32[]{:S(2)}) async-start(bf16[256,10,1152]{2,1,0:T(8,128)(2,1)} %bitcast.126), calls=%async_computation | async-start | bytes 18874368 | tf_op jit(solution)/shard_map/all_to_all | solution.py:28
  34.5 9.0 %copy-start.10 = (s32[512,2,8]{0,2,1:T(8,128)S(1)}, s32[512,2,8]{0,2,1:T(8,128)}, u32[]{:S(2)}) copy-start(s32[512,2,8]{0,2,1:T(8,128)} %param.9) | copy-start | bytes 98308
  194.8 57.3 %copy-start.13 = (s32[4,2]{0,1:T(2,128)S(1)}, s32[4,2]{0,1:T(2,128)}, u32[]{:S(2)}) copy-start(s32[4,2]{0,1:T(2,128)} %param.11) | copy-start | bytes 100
  194.8 60.7 %copy-start.12 = (s32[4,2,1,8]{3,2,1,0:T(1,128)S(1)}, s32[4,2,1,8]{3,2,1,0:T(1,128)}, u32[]{:S(2)}) copy-start(s32[4,2,1,8]{3,2,1,0:T(1,128)} %param.10) | copy-start | bytes 772
  241.9 388.6 %all-to-all-start.1 = ((bf16[512,10,1024]{2,1,0:T(8,128)(2,1)}), bf16[512,10,1024]{2,1,0:T(8,128)(2,1)}, u32[]{:S(2)}, u32[]{:S(2)}) async-start(bf16[512,10,1024]{2,1,0:T(8,128)(2,1)} %copy.45), calls=%async_computation.1 | async-start | bytes 33554432 | tf_op jit(solution)/shard_map/all_to_all | solution.py:41
  251.9 528.6 %reduce-scatter.2.cloned.1.call-start = ((), (), s32[]{:S(2)}) async-start(), calls=%async_computation.3 | async-start | bytes 25165824 | tf_op jit(solution)/shard_map/reduce_scatter | solution.py:59
  292.1 4.1 copy-start.1
  322.4 4.1 copy-start.2
  328.6 4.1 copy-start.3
  332.7 2.3 copy-start.4
  335.1 2.3 copy-start.5
  337.4 2.3 copy-start.6
  744.8 4.7 copy-start.7
  744.8 4.7 copy-start.8
  744.8 5.9 copy-start.9
  756.7 0.7 copy-start.15
  756.7 2.7 copy-start.11
Sparse Core Ops, SparseCore 0:
  756.9 23.5 reduce-scatter.1
where the time goes:
time: 802 us; the launch traced here: 794 us
  waiting for transfers between devices  356 us (44%)
  local copies, waits for them, and re-layouts  323 us (40%)
  other arithmetic  49.5 us (6%)
  starting transfers between devices  27.4 us (3%)
  matrix products  24.3 us (3%)
  between operations  14.2 us (2%)
    all_to_all x1, waiting for transfers between devices, per_device(): lax.all_to_all(outgoing, 'occ', split_axis=0, concat_axis=1, tiled=True)  289 us
    gather x4, local copies, waits for them, and re-layouts, per_device(): outgoing = jnp.take_along_axis(partner_slabs, block_pick, axis=2)  68.7 us
    all_to_all x1, waiting for transfers between devices, per_device(): lax.all_to_all(orbital_major, 'occ', split_axis=0, concat_axis=1, tiled=T...  47.1 us
    slice x5, local copies, waits for them, and re-layouts, per_device(): right_side = arrived[p].reshape(-1, BLK, pair_width)[fit_pos[1]]  44.9 us
    gather x12, local copies, waits for them, and re-layouts, select_blocks(): chosen = blocked[fit_pos][:, :, vir_pos, :]  37.1 us
    dot_general x4, matrix products, per_device(): lax.dot_general(masked.reshape(-1, pair_width), right_side.reshape(-1, pa...  24.3 us
    another operation x4, local copies, waits for them, and re-layouts, select_blocks(): matrix.reshape(matrix.shape[0] // BLK, BLK, matrix.shape[1] // BLK, BLK)  23.7 us
    another operation x4, local copies, waits for them, and re-layouts, per_device(): right_side = arrived[p].reshape(-1, BLK, pair_width)[fit_pos[1]]  23.5 us
  transfers between devices with their start and end apart: 3, of which 3 were waited for; matrix products, arithmetic and copies ran while one was open for 32% of the time, Pallas kernels for 0%

commit v1 on v0

v1 whole, which is shorter than its diff:
```python
import functools

import jax
import jax.numpy as jnp
from jax import lax
from jax.experimental import pallas as pl
from jax.experimental.pallas import tpu as pltpu
from jax.sharding import PartitionSpec as P

BLK = 128
OCC_DEV = 2
PARTNERS = 2
ODB = 9
VB = 8
OFB = 10
FB = 8
LATE = 4
EARLY = ODB - LATE
ROWP = 5
HALF = BLK // 2
F32 = jnp.float32
BF16 = jnp.bfloat16

EARLY_UNITS = (
    [(0, c) for c in range(ODB)]
    + [(1, c) for c in range(ODB)]
    + [(2, c) for c in range(ODB)]
    + [(3, c) for c in range(EARLY)]
)
LATE_UNITS = [(3, c) for c in range(EARLY, ODB)]
EARLY_GROUPS = len(EARLY_UNITS) // 4
LATE_GROUPS = len(LATE_UNITS) // 4
VMEM_LIMIT = 60 * 1024 * 1024


def pack_kernel(pick_ref, rows_ref, early_ref, late_ref, spread):
    owners = early_ref.shape[0]
    for o in range(4):
        units = [(n, c) for n, (q, c) in enumerate(EARLY_UNITS + LATE_UNITS) if q == o]
        for w in range(2):
            picked = jnp.dot(
                pick_ref[o * owners : (o + 1) * owners, :],
                rows_ref[w],
                preferred_element_type=F32,
            )
            for n, c in units:
                spread[n // 4, pl.ds((n % 4) * 2 + w, owners, stride=8), :] = picked[
                    :, c * BLK : (c + 1) * BLK
                ]
    for g in range(EARLY_GROUPS):
        early_ref[:, 0, g] = spread[g].reshape(owners, 8, BLK).astype(BF16)
    for g in range(LATE_GROUPS):
        late_ref[:, 0, g] = spread[EARLY_GROUPS + g].reshape(owners, 8, BLK).astype(BF16)


def pack(pick, rows, owners):
    orbitals, width = rows.shape[1], rows.shape[2]
    groups = (EARLY_GROUPS, LATE_GROUPS)
    return pl.pallas_call(
        pack_kernel,
        grid=(ROWP,),
        in_specs=[
            pl.BlockSpec((4 * owners, orbitals), lambda r: (0, 0)),
            pl.BlockSpec((2, orbitals, width), lambda r: (r, 0, 0)),
        ],
        out_specs=[
            pl.BlockSpec((owners, 1, n, 8, BLK), lambda r: (0, r, 0, 0, 0)) for n in groups
        ],
        out_shape=[
            jax.ShapeDtypeStruct((owners, ROWP, n, 8, BLK), BF16) for n in groups
        ],
        scratch_shapes=[
            pltpu.VMEM((EARLY_GROUPS + LATE_GROUPS, owners * 8, BLK), F32)
        ],
        compiler_params=pltpu.CompilerParams(vmem_limit_bytes=VMEM_LIMIT),
        name="pack",
    )(pick, rows)


def unpack_kernel(order_ref, in_ref, *out_refs, targets):
    groups = in_ref.shape[1]
    for s in range(2):
        part = in_ref[s * 32 : (s + 1) * 32].astype(F32)
        for g in range(groups):
            rows = part[:, g].reshape(256, BLK).astype(BF16)
            sorted_rows = jnp.dot(order_ref[...], rows, preferred_element_type=F32)
            sorted_rows = sorted_rows.astype(BF16)
            for j in range(4):
                which, slot = targets[g * 4 + j]
                out_refs[which][slot, 0, s * HALF : (s + 1) * HALF, :] = sorted_rows[
                    j * HALF : (j + 1) * HALF
                ]


def unpack(order, arrived, counts, targets):
    pairs, groups = arrived.shape[0], arrived.shape[1]
    return pl.pallas_call(
        functools.partial(unpack_kernel, targets=targets),
        grid=(OFB,),
        in_specs=[
            pl.BlockSpec((256, 256), lambda f: (0, 0)),
            pl.BlockSpec((pairs // OFB, groups, 8, BLK), lambda f: (f, 0, 0, 0)),
        ],
        out_specs=[
            pl.BlockSpec((n, 1, BLK, BLK), lambda f: (0, f, 0, 0)) for n in counts
        ],
        out_shape=[jax.ShapeDtypeStruct((n, OFB, BLK, BLK), BF16) for n in counts],
        compiler_params=pltpu.CompilerParams(vmem_limit_bytes=VMEM_LIMIT),
        name="unpack",
    )(order, arrived)


def pair_kernel(
    vir_ref, fit_ref, count_ref, occ_ref, aux_ref, *refs, partner, right_parts
):
    lefts = refs[:2]
    rights = refs[2 : 2 + 2 * len(right_parts)]
    energy_ref, out_ref, left_mat, right_mat = refs[2 + 2 * len(right_parts) :]
    k = pl.program_id(0)
    p = k * PARTNERS + partner
    aux = aux_ref[0]
    fit_count = count_ref[p, 1]
    half_blocks = VB // 2
    for h in range(2):

        @pl.loop(0, FB)
        def _(f):
            at = pl.multiple_of((h * FB + f) * BLK, BLK)
            left_pos = fit_ref[h, p, 0, f]
            right_pos = fit_ref[h, p, 1, f]
            live = f < fit_count
            for v in range(half_blocks):
                c = vir_ref[p, 0, aux * half_blocks + v]
                block = lefts[h][c, left_pos]
                left_mat[pl.ds(at, BLK), v * BLK : (v + 1) * BLK] = jnp.where(
                    live, block, jnp.zeros_like(block)
                )
            for v in range(VB):
                c = vir_ref[p, 1, v]
                where = pl.ds(at, BLK), slice(v * BLK, (v + 1) * BLK)
                start = 0
                for part, size in enumerate(right_parts):
                    source = rights[2 * part + h]

                    @pl.when((c >= start) & (c < start + size))
                    def _(source=source, start=start):
                        right_mat[where] = source[c - start, right_pos]

                    start += size

    live_limit = count_ref[p, 0] * BLK
    occ_sum = (occ_ref[0, p], occ_ref[1, p])
    row_base = aux * half_blocks * BLK
    for v in range(half_blocks):
        row_id = row_base + v * BLK + lax.broadcasted_iota(jnp.int32, (BLK, 1), 0)
        at = pl.multiple_of(row_base + v * BLK, BLK)
        row_energy = energy_ref[0, :, pl.ds(at, BLK)].reshape(BLK, 1)
        product = lax.dot_general(
            left_mat[:, v * BLK : (v + 1) * BLK],
            right_mat[...],
            (((0,), (0,)), ((), ())),
            preferred_element_type=F32,
        )
        denominator = row_energy + energy_ref[0] - occ_sum[0] - occ_sum[1]
        col_id = lax.broadcasted_iota(jnp.int32, (1, VB * BLK), 1)
        live = (row_id < live_limit) & (col_id < live_limit)
        amplitude = jnp.where(live, -product / denominator, 0.0)
        out_ref[0, 0, v * BLK : (v + 1) * BLK, :] = amplitude.astype(BF16)


def pair_products(scalars, lefts, rights, energies, partner):
    right_parts = tuple(r[0].shape[0] for r in rights)
    width = VB * BLK
    left_spec = pl.BlockSpec((ODB, OFB, BLK, BLK), lambda k, *_: (k, 0, 0, 0))
    right_specs = [
        pl.BlockSpec((n, OFB, BLK, BLK), lambda k, *_: (0, 0, 0, 0))
        for n in right_parts
        for _ in range(2)
    ]
    return pl.pallas_call(
        functools.partial(pair_kernel, partner=partner, right_parts=right_parts),
        grid_spec=pltpu.PrefetchScalarGridSpec(
            num_scalar_prefetch=5,
            grid=(OCC_DEV,),
            in_specs=[left_spec, left_spec]
            + right_specs
            + [
                pl.BlockSpec(
                    (1, 1, width), lambda k, *_: (k * PARTNERS + partner, 0, 0)
                )
            ],
            out_specs=pl.BlockSpec((1, 1, width // 2, width), lambda k, *_: (k, 0, 0, 0)),
            scratch_shapes=[
                pltpu.VMEM((2 * FB * BLK, width // 2), BF16),
                pltpu.VMEM((2 * FB * BLK, width), BF16),
            ],
        ),
        out_shape=jax.ShapeDtypeStruct((OCC_DEV, 1, width // 2, width), BF16),
        compiler_params=pltpu.CompilerParams(vmem_limit_bytes=VMEM_LIMIT),
        name="pairs",
    )(*scalars, *lefts, *[x for r in rights for x in r], energies)


def per_device(
    three_index, partners, vir_blocks, fit_blocks, block_counts, virt_energies, occ_energies
):
    owners = lax.axis_size("occ")
    owner = lax.axis_index("occ")
    aux = lax.axis_index("aux")
    pairs_dev = OCC_DEV * PARTNERS
    swap = [(0, 1), (1, 0)]

    rows = jnp.transpose(three_index[0], (1, 0, 2))
    orbitals = jnp.arange(rows.shape[1], dtype=jnp.int32)
    wanted = jnp.concatenate(
        [orbitals.reshape(owners, OCC_DEV).T.reshape(-1), partners.reshape(owners, PARTNERS).T.reshape(-1)]
    )
    pick = (wanted[:, None] == orbitals[None, :]).astype(BF16)
    early, late = pack(pick, rows, owners)

    early = lax.all_to_all(early, "occ", 0, 0, tiled=True)
    late = lax.all_to_all(late, "occ", 0, 0, tiled=True)

    place = jnp.arange(256, dtype=jnp.int32)
    source = (place % HALF) // 2 * 8 + (place // HALF) * 2 + place % 2
    order = (source[:, None] == place[None, :]).astype(BF16)

    targets = [(0, o * ODB + c) for o in range(2) for c in range(ODB)]
    targets += [(1, c) for c in range(ODB)] + [(2, c) for c in range(EARLY)]
    flat = early.reshape(owners * ROWP, EARLY_GROUPS, 8, BLK)
    left, first, second = unpack(order, flat, (2 * ODB, ODB, EARLY), targets)
    flat = late.reshape(owners * ROWP, LATE_GROUPS, 8, BLK)
    (third,) = unpack(order, flat, (LATE,), [(0, c) for c in range(LATE)])

    def both(x):
        return x, lax.ppermute(x, "aux", swap)

    fit_own = fit_blocks[:, :, 0, :]
    fits = jnp.stack(both(fit_own))
    vir = lax.dynamic_slice_in_dim(vir_blocks, owner * pairs_dev, pairs_dev, 0)
    mine = lax.dynamic_slice_in_dim(occ_energies, owner * OCC_DEV, OCC_DEV, 0)
    partner_ids = lax.dynamic_slice_in_dim(partners, owner * PARTNERS, PARTNERS, 0)
    theirs = jnp.sum(
        jnp.where(partner_ids[:, None] == orbitals[None, :], occ_energies[None, :], 0.0), axis=1
    )
    occ_pair = jnp.stack(
        [jnp.repeat(mine, PARTNERS), jnp.concatenate([theirs] * OCC_DEV)]
    )
    scalars = (vir, fits, block_counts, occ_pair, aux.reshape(1))
    energies = virt_energies[:, None, :]

    lefts = both(left)
    out0 = pair_products(scalars, lefts, [both(first)], energies, 0)
    out1 = pair_products(scalars, lefts, [both(second), both(third)], energies, 1)
    out = jnp.concatenate([out0, out1], axis=1)
    return out.reshape(pairs_dev, VB * BLK // 2, VB * BLK)


def solution(mesh):
    return jax.shard_map(
        per_device,
        mesh=mesh,
        in_specs=(
            P("aux", None, "occ", None),
            P(),
            P(),
            P("occ", None, "aux", None),
            P("occ", None),
            P("occ", None),
            P(),
        ),
        out_specs=P("occ", "aux", None),
        check_vma=False,
    )
```

time: 802 us -> 377 us (0.47)
  local copies, waits for them, and re-layouts: 323 us -> 5.4 us
  waiting for transfers between devices: 356 us -> 266 us
  Pallas kernels: 0 us -> 69.5 us
  other arithmetic: 49.5 us -> 7.08 us
  matrix products: 24.3 us -> 0 us
  between operations: 14.2 us -> 0.1 us
    gather x25 -> x0, local copies, waits for them, and re-layouts: 141 us -> none  [the longest x4 68.7 us: per_device(): outgoing = jnp.take_along_axis(partner_slabs, block_pick, axis=2)]
    all_to_all x2, waiting for transfers between devices: 336 us -> 266 us  [the longest x1 231 us: per_device(): early = lax.all_to_all(early, 'occ', 0, 0, tiled=True)]
    pallas_call x0 -> x5, Pallas kernels: none -> 69.5 us  [the longest x2 37.1 us: pair_products(): pl.pallas_call(functools.partial(pair_kernel, partner=partner, right_part...]
    another operation x9 -> x1, local copies, waits for them, and re-layouts: 60.4 us -> 0.08 us  [per_device(): jnp.stack([jnp.repeat(mine, PARTNERS), jnp.concatenate([theirs] * OCC_DEV)])]
    slice x8 -> x0, local copies, waits for them, and re-layouts: 54 us -> none  [the longest x5 44.9 us: per_device(): right_side = arrived[p].reshape(-1, BLK, pair_width)[fit_pos[1]]]
    select_n x14 -> x0, other arithmetic: 34.3 us -> none  [the longest x2 17.3 us: per_device(): partner_slabs = jnp.take(blocked, partner_ids, axis=0)]
    dot_general x4 -> x0, matrix products: 24.3 us -> none  [per_device(): lax.dot_general(masked.reshape(-1, pair_width), right_side.reshape(-1, pa...]
    select_n x2 -> x0, local copies, waits for them, and re-layouts: 22.8 us -> none  [the longest x1 22.7 us: per_device(): outgoing = jnp.take_along_axis(partner_slabs, block_pick, axis=2)]
  transfers between devices with their start and end apart: 3 -> 7, of which waited for: 3 -> 2; matrix products, arithmetic and copies ran while one was open for 32% -> 1% of each run, Pallas kernels for 0% -> 7%
where the time goes in v1:
time: 377 us; the launch traced here: 376 us
  waiting for transfers between devices  266 us (71%)
  Pallas kernels  69.5 us (18%)
  starting transfers between devices  28.4 us (8%)
  other arithmetic  7.08 us (2%)
  local copies, waits for them, and re-layouts  5.4 us (1%)
    all_to_all x1, waiting for transfers between devices, per_device(): early = lax.all_to_all(early, 'occ', 0, 0, tiled=True)  231 us
    pallas_call x2, Pallas kernels, pair_products(): pl.pallas_call(functools.partial(pair_kernel, partner=partner, right_part...  37.1 us
    all_to_all x1, waiting for transfers between devices, per_device(): late = lax.all_to_all(late, 'occ', 0, 0, tiled=True)  34.3 us
    pallas_call x2, Pallas kernels, unpack(): pl.pallas_call(functools.partial(unpack_kernel, targets=targets), grid=(O...  20.4 us
    all_to_all x1, starting transfers between devices, per_device(): early = lax.all_to_all(early, 'occ', 0, 0, tiled=True)  16.8 us
    pallas_call x1, Pallas kernels, pack(): pl.pallas_call(pack_kernel, grid=(ROWP,), in_specs=[pl.BlockSpec((4 * own...  12 us
  transfers between devices with their start and end apart: 7, of which 2 were waited for; matrix products, arithmetic and copies ran while one was open for 1% of the time, Pallas kernels for 7%

profile of v1, /device:TPU:1, one launch (start us, length us, event | category | flops | bytes accessed | tf_op | source)
XLA Modules:
  0.0 376.3 jit_solution(6350113106830131103)
XLA Ops:
  0.0 0.8 reshape.84
  0.9 0.9 fusion.pick_ref
  1.8 12.0 %pack.1 = (bf16[128,5,8,8,128]{4,3,2,1,0:T(8,128)(2,1)}, bf16[128,5,1,8,128]{4,3,2,1,0:T(8,128)(2,1)}) custom-call(bf16[512,256]{1,0:T(8,128)(2,1)} %fusion.pick_ref, bf16[10,256,1152]{2,1,0:T(8,128)(2,1)} %bitcast.16), custom_call_target="tpu_custom_call" | custom-call | tf_op jit(solution)/shard_map/pack/pallas_call | solution.py:59
  13.7 16.8 %all-to-all-start = ((bf16[128,5,8,8,128]{4,3,2,1,0:T(8,128)(2,1)}), bf16[128,5,8,8,128]{4,3,2,1,0:T(8,128)(2,1)}, u32[]{:S(2)}, u32[]{:S(2)}) async-start(bf16[128,5,8,8,128]{4,3,2,1,0:T(8,128)(2,1)} %get-tuple-element.10), calls=%async_computation | async-start | bytes 20971520 | tf_op jit(solution)/shard_map/all_to_all | solution.py:221
  30.6 0.8 fusion.1.order_ref
  31.3 231.5 %all-to-all-done = bf16[128,5,8,8,128]{4,3,2,1,0:T(8,128)(2,1)} async-done(((bf16[128,5,8,8,128]{4,3,2,1,0:T(8,128)(2,1)}), bf16[128,5,8,8,128]{4,3,2,1,0:T(8,128)(2,1)}, u32[]{:S(2)}, u32[]{:S(2)}) %all-to-all-start) | async-done | bytes 10485792 | tf_op jit(solution)/shard_map/all_to_all | solution.py:221
  262.8 13.2 %unpack.2 = (bf16[18,10,128,128]{3,2,1,0:T(8,128)(2,1)}, bf16[9,10,128,128]{3,2,1,0:T(8,128)(2,1)}, bf16[5,10,128,128]{3,2,1,0:T(8,128)(2,1)}) custom-call(bf16[256,256]{1,0:T(8,128)(2,1)} %fusion.1.order_ref, bf16[640,8,8,128]{3,2,1,0:T(8,128)(2,1)} %bitcast.10.in_ref), custom_call_target="tpu_custom_call" | custom-call | tf_op jit(solution)/shard_map/unpack/pallas_call | solution.py:97
  276.0 1.3 collective-permute-start.1
  277.3 7.1 %all-to-all-start.1 = ((bf16[128,5,1,8,128]{4,3,2,1,0:T(8,128)(2,1)}), bf16[128,5,1,8,128]{4,3,2,1,0:T(8,128)(2,1)S(1)}, u32[]{:S(2)}, u32[]{:S(2)}) async-start(bf16[128,5,1,8,128]{4,3,2,1,0:T(8,128)(2,1)} %get-tuple-element.14), calls=%async_computation.1 | async-start | bytes 2621440 | tf_op jit(solution)/shard_map/all_to_all | solution.py:222
  284.4 0.4 collective-permute-start.2
  284.8 0.2 collective-permute-start.3
  285.0 34.3 %all-to-all-done.1 = bf16[128,5,1,8,128]{4,3,2,1,0:T(8,128)(2,1)S(1)} async-done(((bf16[128,5,1,8,128]{4,3,2,1,0:T(8,128)(2,1)}), bf16[128,5,1,8,128]{4,3,2,1,0:T(8,128)(2,1)S(1)}, u32[]{:S(2)}, u32[]{:S(2)}) %all-to-all-start.1) | async-done | bytes 1310752 | tf_op jit(solution)/shard_map/all_to_all | solution.py:222
  319.3 1.1 copy-done.2
  320.4 7.2 %unpack.3.refs_4_ = bf16[4,10,128,128]{3,2,1,0:T(8,128)(2,1)} custom-call(bf16[256,256]{1,0:T(8,128)(2,1)} %fusion.1.order_ref, bf16[640,1,8,128]{3,2,1,0:T(8,128)(2,1)} %bitcast.17), custom_call_target="tpu_custom_call" | custom-call | tf_op jit(solution)/shard_map/unpack/pallas_call | solution.py:97
  327.6 2.4 collective-permute-start.4
  329.9 0.3 collective-permute-start
  330.2 0.1 dynamic_slice.11
  330.3 0.1 dynamic_slice.10
  330.4 0.1 broadcast_in_dim.16
  330.4 0.1 stack_reshape.3
  330.5 0.1 constant_dynamic-slice_fusion
  330.6 0.7 copy.19.vir_ref
  331.3 0.2 fusion.2
  331.5 0.1 maximum_bitcast_fusion
  331.5 0.6 pad_maximum_fusion.1.occ_ref
  332.1 0.6 broadcast_in_dim.28.refs_4_.refs_6_
  332.7 0.6 copy.17.count_ref
  333.4 0.6 pad_add_fusion.fit_ref
  334.0 18.2 %pairs.2 = bf16[2,1,512,1024]{3,2,1,0:T(8,128)(2,1)} custom-call(s32[4,2,8]{2,1,0:T(2,128)} %copy.19.vir_ref, s32[2,4,2,8]{3,2,1,0:T(2,128)} %pad_add_fusion.fit_ref, s32[4,2]{1,0:T(4,128)} %copy.17.count_ref, f32[2,4]{1,0:T(2,128)} %pad_maximum_fusion.1.occ_ref, s32[1]{0:T(128)} %bitcast.4.aux_ref, bf16[18,10,128,128]{3,2,1,0:T(8,128)(2,1)} %get-tuple-element.11.refs_0_, ...), custom_call_target="tpu_custom_call" | custom-call | tf_op jit(solution)/shard_map/pairs/pallas_call | solution.py:180
  352.1 1.2 copy-done.3
  353.3 19.0 %pairs.3 = bf16[2,1,512,1024]{3,2,1,0:T(8,128)(2,1)} custom-call(s32[4,2,8]{2,1,0:T(2,128)} %copy.19.vir_ref, s32[2,4,2,8]{3,2,1,0:T(2,128)} %pad_add_fusion.fit_ref, s32[4,2]{1,0:T(4,128)} %copy.17.count_ref, f32[2,4]{1,0:T(2,128)} %pad_maximum_fusion.1.occ_ref, s32[1]{0:T(128)} %bitcast.4.aux_ref, bf16[18,10,128,128]{3,2,1,0:T(8,128)(2,1)} %get-tuple-element.11.refs_0_, ...), custom_call_target="tpu_custom_call" | custom-call | tf_op jit(solution)/shard_map/pairs/pallas_call | solution.py:180
  372.3 4.0 %pad_maximum_fusion = bf16[2,2,512,1024]{3,2,1,0:T(8,128)(2,1)} fusion(bf16[2,1,512,1024]{3,2,1,0:T(8,128)(2,1)} %pairs.3, bf16[2,1,512,1024]{3,2,1,0:T(8,128)(2,1)S(1)} %copy-done.1), kind=kLoop, calls=%fused_computation | loop fusion | flops 2097152 | bytes 8388608 | tf_op jit(solution)/shard_map/concatenate | solution.py:255
  (25 shorter events, 0.1 us)
Async XLA Ops:
  0.0 330.5 %copy-start = (s32[512,2,8]{0,2,1:T(8,128)S(1)}, s32[512,2,8]{0,2,1:T(8,128)}, u32[]{:S(2)}) copy-start(s32[512,2,8]{0,2,1:T(8,128)} %param.9) | copy-start | bytes 98308
  13.7 249.1 %all-to-all-start = ((bf16[128,5,8,8,128]{4,3,2,1,0:T(8,128)(2,1)}), bf16[128,5,8,8,128]{4,3,2,1,0:T(8,128)(2,1)}, u32[]{:S(2)}, u32[]{:S(2)}) async-start(bf16[128,5,8,8,128]{4,3,2,1,0:T(8,128)(2,1)} %get-tuple-element.10), calls=%async_computation | async-start | bytes 20971520 | tf_op jit(solution)/shard_map/all_to_all | solution.py:221
  275.9 54.0 %copy-start.5 = (s32[4,2,1,8]{3,2,1,0:T(1,128)S(1)}, s32[4,2,1,8]{3,2,1,0:T(1,128)}, u32[]{:S(2)}) copy-start(s32[4,2,1,8]{3,2,1,0:T(1,128)} %param.10) | copy-start | bytes 772
  275.9 54.3 %copy-start.6 = (s32[256]{0:T(256)S(1)}, s32[256]{0:T(256)}, u32[]{:S(2)}) copy-start(s32[256]{0:T(256)} %param.8) | copy-start | bytes 3076
  275.9 54.3 %copy-start.8 = (f32[256]{0:T(256)S(1)}, f32[256]{0:T(256)}, u32[]{:S(2)}) copy-start(f32[256]{0:T(256)} %param.13) | copy-start | bytes 3076
  276.0 56.2 %copy-start.4 = (f32[4,1024]{1,0:T(4,128)S(1)}, f32[4,1024]{1,0:T(4,128)}, u32[]{:S(2)}) copy-start(f32[4,1024]{1,0:T(4,128)} %param.12) | copy-start | bytes 49156
  276.0 56.8 %copy-start.7 = (s32[4,2]{0,1:T(2,128)S(1)}, s32[4,2]{0,1:T(2,128)}, u32[]{:S(2)}) copy-start(s32[4,2]{0,1:T(2,128)} %param.11) | copy-start | bytes 100
  276.0 58.0 %collective-permute-start.1 = (bf16[18,10,128,128]{3,2,1,0:T(8,128)(2,1)}, bf16[18,10,128,128]{3,2,1,0:T(8,128)(2,1)}, u32[]{:S(2)}, u32[]{:S(2)}) collective-permute-start(bf16[18,10,128,128]{3,2,1,0:T(8,128)(2,1)} %get-tuple-element.11.refs_0_), channel_id=1, source_target_pairs={{0,1},{1,0},{2,3},{3,2},{4,5},{5,4},{6,7},{7,6},{8,9},{9,8},{10,11... | collective-permute-start | bytes 17694728 | tf_op jit(solution)/shard_map/ppermute | solution.py:236
  277.3 42.0 %all-to-all-start.1 = ((bf16[128,5,1,8,128]{4,3,2,1,0:T(8,128)(2,1)}), bf16[128,5,1,8,128]{4,3,2,1,0:T(8,128)(2,1)S(1)}, u32[]{:S(2)}, u32[]{:S(2)}) async-start(bf16[128,5,1,8,128]{4,3,2,1,0:T(8,128)(2,1)} %get-tuple-element.14), calls=%async_computation.1 | async-start | bytes 2621440 | tf_op jit(solution)/shard_map/all_to_all | solution.py:222
  284.4 49.6 %collective-permute-start.2 = (bf16[9,10,128,128]{3,2,1,0:T(8,128)(2,1)}, bf16[9,10,128,128]{3,2,1,0:T(8,128)(2,1)}, u32[]{:S(2)}, u32[]{:S(2)}) collective-permute-start(bf16[9,10,128,128]{3,2,1,0:T(8,128)(2,1)} %get-tuple-element.12.refs_2_), channel_id=1, source_target_pairs={{0,1},{1,0},{2,3},{3,2},{4,5},{5,4},{6,7},{7,6},{8,9},{9,8},{10,11... | collective-permute-start | bytes 8847368 | tf_op jit(solution)/shard_map/ppermute | solution.py:236
  284.8 67.3 %collective-permute-start.3 = (bf16[5,10,128,128]{3,2,1,0:T(8,128)(2,1)}, bf16[5,10,128,128]{3,2,1,0:T(8,128)(2,1)S(1)}, u32[]{:S(2)}, u32[]{:S(2)}) collective-permute-start(bf16[5,10,128,128]{3,2,1,0:T(8,128)(2,1)} %get-tuple-element.13.refs_2_), channel_id=1, source_target_pairs={{0,1},{1,0},{2,3},{3,2},{4,5},{5,4},{6,7},{7,6},{8,9},{9,8},{10,11... | collective-permute-start | bytes 4915208 | tf_op jit(solution)/shard_map/ppermute | solution.py:236
  319.3 1.1 copy-start.2
  327.6 24.6 %collective-permute-start.4 = (bf16[4,10,128,128]{3,2,1,0:T(8,128)(2,1)}, bf16[4,10,128,128]{3,2,1,0:T(8,128)(2,1)}, u32[]{:S(2)}, u32[]{:S(2)}) collective-permute-start(bf16[4,10,128,128]{3,2,1,0:T(8,128)(2,1)} %unpack.3.refs_4_), channel_id=1, source_target_pairs={{0,1},{1,0},{2,3},{3,2},{4,5},{5,4},{6,7},{7,6},{8,9},{9,8},{10,11... | collective-permute-start | bytes 3932168 | tf_op jit(solution)/shard_map/ppermute | solution.py:236
  329.9 3.4 collective-permute-start
  352.1 20.2 %copy-start.1 = (bf16[2,1,512,1024]{3,2,1,0:T(8,128)(2,1)S(1)}, bf16[2,1,512,1024]{3,2,1,0:T(8,128)(2,1)}, u32[]{:S(2)}) copy-start(bf16[2,1,512,1024]{3,2,1,0:T(8,128)(2,1)} %pairs.2) | copy-start | bytes 6291460
  352.1 1.2 copy-start.3

commit v2 on v0

v2 whole, which is shorter than its diff:
```python
import functools

import jax
import jax.numpy as jnp
from jax import lax
from jax.experimental import pallas as pl
from jax.experimental.pallas import tpu as pltpu
from jax.sharding import PartitionSpec as P

BLK = 128
OCC_DEV = 2
PARTNERS = 2
ODB = 9
VB = 8
OFB = 10
FB = 8
LATE = 4
EARLY = ODB - LATE
ROWP = 5
HALF = BLK // 2
F32 = jnp.float32
BF16 = jnp.bfloat16

EARLY_UNITS = (
    [(0, c) for c in range(ODB)]
    + [(1, c) for c in range(ODB)]
    + [(2, c) for c in range(ODB)]
    + [(3, c) for c in range(EARLY)]
)
LATE_UNITS = [(3, c) for c in range(EARLY, ODB)]
EARLY_GROUPS = len(EARLY_UNITS) // 4
VMEM_LIMIT = 60 * 1024 * 1024


def pack_kernel(pick_ref, rows_ref, early_ref, late_ref, spread):
    owners = early_ref.shape[0]
    for o in range(4):
        units = [(n, c) for n, (q, c) in enumerate(EARLY_UNITS + LATE_UNITS) if q == o]
        for w in range(2):
            picked = jnp.dot(
                pick_ref[o * owners : (o + 1) * owners, :],
                rows_ref[w],
                preferred_element_type=F32,
            )
            for n, c in units:
                spread[n // 4, pl.ds((n % 4) * 2 + w, owners, stride=8), :] = picked[
                    :, c * BLK : (c + 1) * BLK
                ]
    for g in range(EARLY_GROUPS):
        early_ref[:, 0, g] = spread[g].reshape(owners, 8, BLK).astype(BF16)
    late_ref[:, 0] = spread[EARLY_GROUPS].reshape(owners, 8, BLK).astype(BF16)


def pack(pick, rows, owners):
    orbitals, width = rows.shape[1], rows.shape[2]
    return pl.pallas_call(
        pack_kernel,
        grid=(ROWP,),
        in_specs=[
            pl.BlockSpec((4 * owners, orbitals), lambda r: (0, 0)),
            pl.BlockSpec((2, orbitals, width), lambda r: (r, 0, 0)),
        ],
        out_specs=[
            pl.BlockSpec((owners, 1, EARLY_GROUPS, 8, BLK), lambda r: (0, r, 0, 0, 0)),
            pl.BlockSpec((owners, 1, 8, BLK), lambda r: (0, r, 0, 0)),
        ],
        out_shape=[
            jax.ShapeDtypeStruct((owners, ROWP, EARLY_GROUPS, 8, BLK), BF16),
            jax.ShapeDtypeStruct((owners, ROWP, 8, BLK), BF16),
        ],
        scratch_shapes=[pltpu.VMEM((EARLY_GROUPS + 1, owners * 8, BLK), F32)],
        compiler_params=pltpu.CompilerParams(vmem_limit_bytes=24 * 1024 * 1024),
        name="pack",
    )(pick, rows)


def sorted_rows(order, block):
    rows = jnp.concatenate(
        [b.astype(F32).reshape(-1, BLK).astype(BF16) for b in block], axis=1
    )
    return jnp.dot(order, rows, preferred_element_type=F32)


def row_energies(energy_ref, p, base):
    parts = [
        energy_ref[p, :, pl.ds(pl.multiple_of(base + i * BLK, BLK), BLK)].reshape(BLK, 1)
        for i in range(VB // 2)
    ]
    return jnp.concatenate(parts, axis=0)


def amplitudes(product, v, p, count_ref, occ_ref, energy_ref, base, row_energy):
    at = pl.multiple_of(v * BLK, BLK)
    live_limit = count_ref[p, 0] * BLK
    denominator = (
        row_energy + energy_ref[p, :, pl.ds(at, BLK)] - occ_ref[0, p] - occ_ref[1, p]
    )
    row = base + lax.broadcasted_iota(jnp.int32, (product.shape[0], 1), 0)
    live = (row < live_limit) & (at < live_limit)
    return jnp.where(live, -product / denominator, 0.0).astype(BF16)


def middle_kernel(
    vir_ref, fit_ref, count_ref, occ_ref, aux_ref, early_ref,
    order_ref, own_ref, other_ref, energy_ref,
    out_ref, left1_ref,
    blocks, first, second, left0,
):
    step = pl.program_id(0)
    pairs = own_ref.shape[0] // 2
    half_blocks = VB // 2
    rows = half_blocks * BLK
    aux = aux_ref[0]
    for h, source in enumerate((own_ref, other_ref)):
        at = pl.multiple_of((h * OFB + step) * BLK, BLK)
        for g in range(0, EARLY_GROUPS, 2):
            halves = [
                sorted_rows(
                    order_ref[...],
                    [source[s * pairs : (s + 1) * pairs, g + i] for i in range(2)],
                )
                for s in range(2)
            ]
            for i in range(2):
                for j in range(4):
                    o, c = EARLY_UNITS[(g + i) * 4 + j]
                    block = jnp.concatenate(
                        [x[j * HALF : (j + 1) * HALF, i * BLK : (i + 1) * BLK] for x in halves],
                        axis=0,
                    ).astype(BF16)
                    if o < 2:
                        blocks[h, o * ODB + c, step] = block.T
                    elif o == 2:
                        first[pl.ds(at, BLK), c * BLK : (c + 1) * BLK] = block
                    else:
                        second[pl.ds(at, BLK), c * BLK : (c + 1) * BLK] = block

    @pl.when(step == pl.num_programs(0) - 1)
    def _():
        for m, left in enumerate((left0, left1_ref)):
            left[...] = jnp.zeros_like(left)
            for k in range(OCC_DEV):
                p = k * PARTNERS + m
                for h in range(2):

                    @pl.loop(0, count_ref[p, 1])
                    def _(f, p=p, k=k, h=h, left=left):
                        left_pos = fit_ref[h, p, 0, f]
                        at = pl.multiple_of((h * OFB + fit_ref[h, p, 1, f]) * BLK, BLK)
                        for v in range(half_blocks):
                            c = vir_ref[p, 0, aux * half_blocks + v]
                            where = slice(k * rows + v * BLK, k * rows + (v + 1) * BLK)
                            left[where, pl.ds(at, BLK)] = blocks[h, k * ODB + c, left_pos]

        for m, (left, right, turns) in enumerate(
            ((left0, first, VB // 2), (left1_ref, second, early_ref.shape[1] // 2))
        ):

            @pl.loop(0, OCC_DEV * turns)
            def _(i, m=m, left=left, right=right, turns=turns):
                k = i // turns
                p = k * PARTNERS + m
                base = aux * rows
                row_energy = row_energies(energy_ref, p, base)
                at = [(i % turns) * 2 + n for n in range(2)]
                if m == 1:
                    at = [early_ref[p, n] for n in at]
                columns = [pl.multiple_of(vir_ref[p, 1, v] * BLK, BLK) for v in at]
                product = jnp.dot(
                    left[pl.ds(pl.multiple_of(k * rows, rows), rows), :],
                    jnp.concatenate([right[:, pl.ds(c, BLK)] for c in columns], axis=1),
                    preferred_element_type=F32,
                )
                for n, v in enumerate(at):
                    out_ref[p, :, pl.ds(pl.multiple_of(v * BLK, BLK), BLK)] = amplitudes(
                        product[:, n * BLK : (n + 1) * BLK],
                        v, p, count_ref, occ_ref, energy_ref, base, row_energy,
                    )


def middle(scalars, order, own, other, energies):
    pairs = own.shape[0]
    depth = 2 * OFB * BLK
    rows = VB // 2 * BLK
    raw = pl.BlockSpec((pairs // OFB, EARLY_GROUPS, 8, BLK), lambda f, *_: (f, 0, 0, 0))
    out = jax.ShapeDtypeStruct((OCC_DEV * PARTNERS, rows, VB * BLK), BF16)
    left1 = jax.ShapeDtypeStruct((OCC_DEV * rows, depth), BF16)
    return pl.pallas_call(
        middle_kernel,
        grid_spec=pltpu.PrefetchScalarGridSpec(
            num_scalar_prefetch=len(scalars),
            grid=(OFB,),
            in_specs=[
                pl.BlockSpec(order.shape, lambda f, *_: (0, 0)),
                raw,
                raw,
                pl.BlockSpec(energies.shape, lambda f, *_: (0, 0, 0)),
            ],
            out_specs=[
                pl.BlockSpec(out.shape, lambda f, *_: (0, 0, 0)),
                pl.BlockSpec(left1.shape, lambda f, *_: (0, 0)),
            ],
            scratch_shapes=[
                pltpu.VMEM((2, OCC_DEV * ODB, OFB, BLK, BLK), BF16),
                pltpu.VMEM((depth, ODB * BLK), BF16),
                pltpu.VMEM((depth, EARLY * BLK), BF16),
                pltpu.VMEM(left1.shape, BF16),
            ],
        ),
        out_shape=[out, left1],
        compiler_params=pltpu.CompilerParams(vmem_limit_bytes=VMEM_LIMIT),
        name="middle",
    )(*scalars, order, own, other, energies)


def late_kernel(
    vir_ref, late_ref, count_ref, occ_ref, aux_ref,
    order_ref, left_ref, own_ref, other_ref, energy_ref, before_ref,
    out_ref, right,
):
    k = pl.program_id(0)
    p = k * PARTNERS + 1
    group = order_ref.shape[0] // 8
    chunks = own_ref.shape[0] // group

    @pl.when(k == 0)
    def _():
        for h, source in enumerate((own_ref, other_ref)):
            for s in range(0, chunks, 4):
                done = sorted_rows(
                    order_ref[...],
                    [source[(s + i) * group : (s + i + 1) * group] for i in range(4)],
                ).astype(BF16)
                for i in range(4):
                    at = (h * chunks + s + i) * HALF
                    for j in range(4):
                        right[at : at + HALF, j * BLK : (j + 1) * BLK] = done[
                            j * HALF : (j + 1) * HALF, i * BLK : (i + 1) * BLK
                        ]

    out_ref[...] = before_ref[...]
    base = aux_ref[0] * left_ref.shape[0]
    row_energy = row_energies(energy_ref, p, base)
    for turn in range(LATE // 2):
        at = [late_ref[p, turn * 2 + n] for n in range(2)]
        columns = [pl.multiple_of((vir_ref[p, 1, v] - EARLY) * BLK, BLK) for v in at]
        product = jnp.dot(
            left_ref[...],
            jnp.concatenate([right[:, pl.ds(c, BLK)] for c in columns], axis=1),
            preferred_element_type=F32,
        )
        for n, v in enumerate(at):
            out_ref[0, :, pl.ds(pl.multiple_of(v * BLK, BLK), BLK)] = amplitudes(
                product[:, n * BLK : (n + 1) * BLK],
                v, p, count_ref, occ_ref, energy_ref, base, row_energy,
            )


def late_products(scalars, order, left1, own, other, energies, before):
    depth = left1.shape[1]
    rows = left1.shape[0] // OCC_DEV
    out = pl.BlockSpec((1, rows, VB * BLK), lambda k, *_: (k * PARTNERS + 1, 0, 0))
    return pl.pallas_call(
        late_kernel,
        grid_spec=pltpu.PrefetchScalarGridSpec(
            num_scalar_prefetch=len(scalars),
            grid=(OCC_DEV,),
            in_specs=[
                pl.BlockSpec(order.shape, lambda k, *_: (0, 0)),
                pl.BlockSpec((rows, depth), lambda k, *_: (k, 0)),
                pl.BlockSpec(own.shape, lambda k, *_: (0, 0, 0)),
                pl.BlockSpec(other.shape, lambda k, *_: (0, 0, 0)),
                pl.BlockSpec(energies.shape, lambda k, *_: (0, 0, 0)),
                out,
            ],
            out_specs=out,
            scratch_shapes=[pltpu.VMEM((depth, LATE * BLK), BF16)],
        ),
        out_shape=jax.ShapeDtypeStruct(before.shape, BF16),
        input_output_aliases={len(scalars) + 5: 0},
        compiler_params=pltpu.CompilerParams(vmem_limit_bytes=32 * 1024 * 1024),
        name="late",
    )(*scalars, order, left1, own, other, energies, before)


def per_device(
    three_index, partners, vir_blocks, fit_blocks, block_counts, virt_energies, occ_energies
):
    owners = lax.axis_size("occ")
    owner = lax.axis_index("occ")
    aux = lax.axis_index("aux").reshape(1)
    pairs_dev = OCC_DEV * PARTNERS

    def swap(x):
        return lax.ppermute(x, "aux", [(0, 1), (1, 0)])

    rows = jnp.transpose(three_index[0], (1, 0, 2))
    orbitals = jnp.arange(rows.shape[1], dtype=jnp.int32)
    wanted = jnp.concatenate(
        [orbitals.reshape(owners, OCC_DEV).T.reshape(-1), partners.reshape(owners, PARTNERS).T.reshape(-1)]
    )
    pick = (wanted[:, None] == orbitals[None, :]).astype(BF16)
    early, late = pack(pick, rows, owners)
    early = lax.all_to_all(early, "occ", 0, 0, tiled=True)
    late = lax.all_to_all(late, "occ", 0, 0, tiled=True)

    fit_own = fit_blocks[:, :, 0, :]
    fits = jnp.stack([fit_own, swap(fit_own)])
    vir = lax.dynamic_slice_in_dim(vir_blocks, owner * pairs_dev, pairs_dev, 0)
    numbers = jnp.arange(VB, dtype=jnp.int32)
    is_late = vir[:, 1, :] >= EARLY

    def listed(flags, length):
        upto = numbers[None, :] <= numbers[:, None]
        rank = jnp.sum(jnp.where(flags[:, None, :] & upto, 1, 0), axis=2)
        total = rank[:, -1:]
        nth = jnp.minimum(jnp.arange(1, length + 1, dtype=jnp.int32), total)
        hit = flags[:, None, :] & (rank[:, None, :] == nth[:, :, None])
        return jnp.sum(jnp.where(hit, numbers, 0), axis=2)

    early_at = listed(~is_late, EARLY + 1)
    late_at = listed(is_late, LATE)
    mine = lax.dynamic_slice_in_dim(occ_energies, owner * OCC_DEV, OCC_DEV, 0)
    partner_ids = lax.dynamic_slice_in_dim(partners, owner * PARTNERS, PARTNERS, 0)
    theirs = jnp.sum(
        jnp.where(partner_ids[:, None] == orbitals[None, :], occ_energies[None, :], 0.0), axis=1
    )
    occ_pair = jnp.stack([jnp.repeat(mine, PARTNERS), jnp.concatenate([theirs] * OCC_DEV)])
    energies = virt_energies[:, None, :]

    place = jnp.arange(256, dtype=jnp.int32)
    source = (place % HALF) // 2 * 8 + (place // HALF) * 2 + place % 2
    order = (source[:, None] == place[None, :]).astype(BF16)

    early = early.reshape(owners * ROWP, EARLY_GROUPS, 8, BLK)
    scalars = (vir, fits, block_counts, occ_pair, aux, early_at)
    out, left1 = middle(scalars, order, early, swap(early), energies)
    late, out = lax.optimization_barrier((late, out))
    late = late.reshape(owners * ROWP, 8, BLK)
    scalars = (vir, late_at, block_counts, occ_pair, aux)
    return late_products(scalars, order, left1, late, swap(late), energies, out)


def solution(mesh):
    return jax.shard_map(
        per_device,
        mesh=mesh,
        in_specs=(
            P("aux", None, "occ", None),
            P(),
            P(),
            P("occ", None, "aux", None),
            P("occ", None),
            P("occ", None),
            P(),
        ),
        out_specs=P("occ", "aux", None),
        check_vma=False,
    )
```

time: 802 us -> 326 us (0.41); the launches traced: 794 us -> 326 us
  waiting for transfers between devices: 356 us -> 6.26 us
  local copies, waits for them, and re-layouts: 323 us -> 9.29 us
  blocking collectives: 0 us -> 246 us
  Pallas kernels: 0 us -> 50 us
  other arithmetic: 49.5 us -> 3.19 us
  matrix products: 24.3 us -> 0 us
  starting transfers between devices: 27.4 us -> 11.7 us
  between operations: 14.2 us -> 0.16 us
    all_to_all x2 -> x1, waiting for transfers between devices: 336 us -> 0.01 us  [per_device(): late = lax.all_to_all(late, 'occ', 0, 0, tiled=True)]
    all_to_all x0 -> x1, blocking collectives: none -> 246 us  [per_device(): early = lax.all_to_all(early, 'occ', 0, 0, tiled=True)]
    gather x25 -> x0, local copies, waits for them, and re-layouts: 141 us -> none  [the longest x4 68.7 us: per_device(): outgoing = jnp.take_along_axis(partner_slabs, block_pick, axis=2)]
    another operation x9 -> x1, local copies, waits for them, and re-layouts: 60.4 us -> 0.08 us  [per_device(): jnp.stack([jnp.repeat(mine, PARTNERS), jnp.concatenate([theirs] * OCC_DEV)])]
    slice x8 -> x1, local copies, waits for them, and re-layouts: 54 us -> 0.22 us  [listed(): total = rank[:, -1:]]
    pallas_call x0 -> x3, Pallas kernels: none -> 50 us  [the longest x1 33 us: middle(): pl.pallas_call(middle_kernel, grid_spec=pltpu.PrefetchScalarGridSpec(num_...]
    select_n x14 -> x0, other arithmetic: 34.3 us -> none  [the longest x2 17.3 us: per_device(): partner_slabs = jnp.take(blocked, partner_ids, axis=0)]
    dot_general x4 -> x0, matrix products: 24.3 us -> none  [per_device(): lax.dot_general(masked.reshape(-1, pair_width), right_side.reshape(-1, pa...]
  transfers between devices with their start and end apart: 3 -> 4, of which waited for: 3 -> 2; matrix products, arithmetic and copies ran while one was open for 32% -> 2% of each run, Pallas kernels for 0% -> 10%
where the time goes in v2:
time: 326 us
  blocking collectives  246 us (75%)
  Pallas kernels  50 us (15%)
  starting transfers between devices  11.7 us (4%)
  local copies, waits for them, and re-layouts  9.29 us (3%)
  waiting for transfers between devices  6.26 us (2%)
    all_to_all x1, blocking collectives, per_device(): early = lax.all_to_all(early, 'occ', 0, 0, tiled=True)  246 us
    pallas_call x1, Pallas kernels, middle(): pl.pallas_call(middle_kernel, grid_spec=pltpu.PrefetchScalarGridSpec(num_...  33 us
    pallas_call x1, Pallas kernels, pack(): pl.pallas_call(pack_kernel, grid=(ROWP,), in_specs=[pl.BlockSpec((4 * own...  9.57 us
    pallas_call x1, Pallas kernels, late_products(): pl.pallas_call(late_kernel, grid_spec=pltpu.PrefetchScalarGridSpec(num_sc...  7.45 us
    all_to_all x1, starting transfers between devices, per_device(): late = lax.all_to_all(late, 'occ', 0, 0, tiled=True)  6.78 us
    unnamed x32, local copies, waits for them, and re-layouts  6.59 us
  transfers between devices with their start and end apart: 4, of which 2 were waited for; matrix products, arithmetic and copies ran while one was open for 2% of the time, Pallas kernels for 10%

profile of v2, /device:TPU:1, one launch (start us, length us, event | category | flops | bytes accessed | tf_op | source)
XLA Modules:
  0.0 326.2 jit_solution(4328287659131082123)
XLA Ops:
  0.0 0.8 reshape.161
  0.9 0.2 fusion.pick_ref
  1.1 2.7 copy-done.1
  3.7 9.6 %pack.1 = (bf16[128,5,8,8,128]{4,3,2,1,0:T(8,128)(2,1)S(1)}, bf16[128,5,8,128]{3,2,1,0:T(8,128)(2,1)}) custom-call(bf16[512,256]{1,0:T(8,128)(2,1)S(1)} %fusion.pick_ref, bf16[10,256,1152]{2,1,0:T(8,128)(2,1)S(1)} %bitcast.21), custom_call_target="tpu_custom_call" | custom-call | tf_op jit(solution)/shard_map/pack/pallas_call | solution.py:56
  13.3 245.7 %all_to_all.10 = bf16[128,5,8,8,128]{4,3,2,1,0:T(8,128)(2,1)} all-to-all(bf16[128,5,8,8,128]{4,3,2,1,0:T(8,128)(2,1)S(1)} %get-tuple-element.11), channel_id=1, replica_groups=mesh['occ'=128,'aux'=2] {'occ'}, dimensions={0} | all-to-all | bytes 20971520 | tf_op jit(solution)/shard_map/all_to_all | solution.py:304
  259.0 4.2 %collective-permute-start.1 = (bf16[640,8,8,128]{3,2,1,0:T(8,128)(2,1)}, bf16[640,8,8,128]{3,2,1,0:T(8,128)(2,1)}, u32[]{:S(2)}, u32[]{:S(2)}) collective-permute-start(bf16[640,8,8,128]{3,2,1,0:T(8,128)(2,1)} %bitcast.10.own_ref), channel_id=1, source_target_pairs={{0,1},{1,0},{2,3},{3,2},{4,5},{5,4},{6,7},{7,6},{8,9},{9,8},{10,11... | collective-permute-start | bytes 31457288 | tf_op jit(solution)/shard_map/ppermute | solution.py:295
  263.2 6.8 %all-to-all-start.1 = ((bf16[128,5,8,128]{3,2,1,0:T(8,128)(2,1)}), bf16[128,5,8,128]{3,2,1,0:T(8,128)(2,1)S(1)}, u32[]{:S(2)}, u32[]{:S(2)}) async-start(bf16[128,5,8,128]{3,2,1,0:T(8,128)(2,1)} %get-tuple-element.13), calls=%async_computation.1 | async-start | bytes 2621440 | tf_op jit(solution)/shard_map/all_to_all | solution.py:305
  270.0 0.4 collective-permute-start
  270.3 0.1 dynamic_slice.11
  270.4 0.1 dynamic_slice.10
  270.5 0.1 stack_reshape.3
  270.7 0.1 copy.32.vir_ref
  270.9 0.2 fusion.2
  271.0 0.1 maximum_bitcast_fusion
  271.1 0.5 pad_maximum_fusion.occ_ref
  271.7 0.2 select_reduce_fusion
  271.9 0.2 slice_reduce_fusion
  272.2 0.3 select_reduce_fusion.2
  272.4 0.8 fusion.1.order_ref
  273.2 0.6 copy.29.count_ref
  273.8 0.6 copy.28.early_ref
  274.5 0.6 broadcast_in_dim.76.energy_ref
  275.1 3.9 %collective-permute-done = s32[4,2,8]{2,1,0:T(2,128)S(1)} collective-permute-done((s32[4,2,8]{2,1,0:T(2,128)S(1)}, s32[4,2,8]{2,1,0:T(2,128)S(1)}, u32[]{:S(2)}, u32[]{:S(2)}) %collective-permute-start) | collective-permute-done | bytes 288 | tf_op jit(solution)/shard_map/ppermute | solution.py:295
  278.9 0.6 pad_add_fusion.fit_ref
  279.6 33.0 %middle.1 = (bf16[4,512,1024]{2,1,0:T(8,128)(2,1)}, bf16[1024,2560]{1,0:T(8,128)(2,1)}) custom-call(s32[4,2,8]{2,1,0:T(2,128)} %copy-done.5, s32[2,4,2,8]{3,2,1,0:T(2,128)} %pad_add_fusion.fit_ref, s32[4,2]{1,0:T(4,128)} %copy.29.count_ref, f32[2,4]{1,0:T(2,128)} %pad_maximum_fusion.occ_ref, s32[1]{0:T(128)} %bitcast.1.aux_ref, s32[4,6]{1,0:T(4,128)} %copy.28.early_ref, ...), custom_call_target="tpu_custom_call" | custom-call | tf_op jit(solution)/shard_map/middle/pallas_call | solution.py:188
  312.6 0.4 collective-permute-start.2
  312.9 0.1 broadcast_minimum_fusion.1
  313.0 0.2 select_reduce_fusion.3.late_ref
  313.2 2.4 collective-permute-done.2.other_ref
  315.6 2.5 copy-done.2
  318.1 0.7 copy-done.6
  318.8 7.4 %late.1 = bf16[4,512,1024]{2,1,0:T(8,128)(2,1)} custom-call(s32[4,2,8]{2,1,0:T(2,128)S(1)} %copy-done.6, s32[4,4]{1,0:T(4,128)S(1)} %select_reduce_fusion.3.late_ref, s32[4,2]{1,0:T(4,128)S(1)} %copy-done.7, f32[2,4]{1,0:T(2,128)S(1)} %copy-done.8, s32[1]{0:T(128)} %bitcast.1.aux_ref, ...), custom_call_target="tpu_custom_call", output_to_operand_aliasing={{}: (10, {})} | custom-call | tf_op jit(solution)/shard_map/late/pallas_call | solution.py:263
  (40 shorter events, 0.4 us)
Async XLA Ops:
  0.0 270.6 %copy-start = (s32[512,2,8]{0,2,1:T(8,128)S(1)}, s32[512,2,8]{0,2,1:T(8,128)}, u32[]{:S(2)}) copy-start(s32[512,2,8]{0,2,1:T(8,128)} %param.9) | copy-start | bytes 98308
  1.1 2.7 copy-start.1
  13.3 256.6 %copy-start.10 = (s32[4,2,1,8]{3,2,1,0:T(1,128)S(1)}, s32[4,2,1,8]{3,2,1,0:T(1,128)}, u32[]{:S(2)}) copy-start(s32[4,2,1,8]{3,2,1,0:T(1,128)} %param.10) | copy-start | bytes 772
  13.3 257.0 %copy-start.11 = (s32[256]{0:T(256)S(1)}, s32[256]{0:T(256)}, u32[]{:S(2)}) copy-start(s32[256]{0:T(256)} %param.8) | copy-start | bytes 3076
  13.3 257.1 %copy-start.13 = (f32[256]{0:T(256)S(1)}, f32[256]{0:T(256)}, u32[]{:S(2)}) copy-start(f32[256]{0:T(256)} %param.13) | copy-start | bytes 3076
  13.3 259.9 %copy-start.12 = (s32[4,2]{0,1:T(2,128)S(1)}, s32[4,2]{0,1:T(2,128)}, u32[]{:S(2)}) copy-start(s32[4,2]{0,1:T(2,128)} %param.11) | copy-start | bytes 100
  13.3 261.1 %copy-start.9 = (f32[4,1024]{1,0:T(4,128)S(1)}, f32[4,1024]{1,0:T(4,128)}, u32[]{:S(2)}) copy-start(f32[4,1024]{1,0:T(4,128)} %param.12) | copy-start | bytes 49156
  259.0 20.5 %collective-permute-start.1 = (bf16[640,8,8,128]{3,2,1,0:T(8,128)(2,1)}, bf16[640,8,8,128]{3,2,1,0:T(8,128)(2,1)}, u32[]{:S(2)}, u32[]{:S(2)}) collective-permute-start(bf16[640,8,8,128]{3,2,1,0:T(8,128)(2,1)} %bitcast.10.own_ref), channel_id=1, source_target_pairs={{0,1},{1,0},{2,3},{3,2},{4,5},{5,4},{6,7},{7,6},{8,9},{9,8},{10,11... | collective-permute-start | bytes 31457288 | tf_op jit(solution)/shard_map/ppermute | solution.py:295
  263.2 49.4 %all-to-all-start.1 = ((bf16[128,5,8,128]{3,2,1,0:T(8,128)(2,1)}), bf16[128,5,8,128]{3,2,1,0:T(8,128)(2,1)S(1)}, u32[]{:S(2)}, u32[]{:S(2)}) async-start(bf16[128,5,8,128]{3,2,1,0:T(8,128)(2,1)} %get-tuple-element.13), calls=%async_computation.1 | async-start | bytes 2621440 | tf_op jit(solution)/shard_map/all_to_all | solution.py:305
  270.0 9.0 %collective-permute-start = (s32[4,2,8]{2,1,0:T(2,128)S(1)}, s32[4,2,8]{2,1,0:T(2,128)S(1)}, u32[]{:S(2)}, u32[]{:S(2)}) collective-permute-start(s32[4,2,8]{2,1,0:T(2,128)S(1)} %bitcast.30), channel_id=1, source_target_pairs={{0,1},{1,0},{2,3},{3,2},{4,5},{5,4},{6,7},{7,6},{8,9},{9,8},{10,11... | collective-permute-start | bytes 776 | tf_op jit(solution)/shard_map/ppermute | solution.py:295
  270.8 8.7 %copy-start.5 = (s32[4,2,8]{2,1,0:T(2,128)}, s32[4,2,8]{2,1,0:T(2,128)S(1)}, u32[]{:S(2)}) copy-start(s32[4,2,8]{2,1,0:T(2,128)S(1)} %copy.32.vir_ref) | copy-start | bytes 772
  279.5 36.0 %copy-start.3 = (bf16[256,256]{1,0:T(8,128)(2,1)S(1)}, bf16[256,256]{1,0:T(8,128)(2,1)}, u32[]{:S(2)}) copy-start(bf16[256,256]{1,0:T(8,128)(2,1)} %fusion.1.order_ref) | copy-start | bytes 393220
  279.5 36.1 %copy-start.4 = (f32[4,1,1024]{2,1,0:T(1,128)S(1)}, f32[4,1,1024]{2,1,0:T(1,128)}, u32[]{:S(2)}) copy-start(f32[4,1,1024]{2,1,0:T(1,128)} %broadcast_in_dim.76.energy_ref) | copy-start | bytes 49156
  279.6 36.0 %copy-start.7 = (s32[4,2]{1,0:T(4,128)S(1)}, s32[4,2]{1,0:T(4,128)}, u32[]{:S(2)}) copy-start(s32[4,2]{1,0:T(4,128)} %copy.29.count_ref) | copy-start | bytes 100
  279.6 36.0 %copy-start.8 = (f32[2,4]{1,0:T(2,128)S(1)}, f32[2,4]{1,0:T(2,128)}, u32[]{:S(2)}) copy-start(f32[2,4]{1,0:T(2,128)} %pad_maximum_fusion.occ_ref) | copy-start | bytes 100
  312.6 3.0 collective-permute-start.2
  315.6 2.5 copy-start.2
  318.1 0.7 copy-start.6

commit v3 on v2

--- a/solution.py
+++ b/solution.py
@@ -29,23 +29,16 @@
 )
 LATE_UNITS = [(3, c) for c in range(EARLY, ODB)]
 EARLY_GROUPS = len(EARLY_UNITS) // 4
-VMEM_LIMIT = 60 * 1024 * 1024
 
 
 def pack_kernel(pick_ref, rows_ref, early_ref, late_ref, spread):
     owners = early_ref.shape[0]
-    for o in range(4):
-        units = [(n, c) for n, (q, c) in enumerate(EARLY_UNITS + LATE_UNITS) if q == o]
-        for w in range(2):
-            picked = jnp.dot(
-                pick_ref[o * owners : (o + 1) * owners, :],
-                rows_ref[w],
-                preferred_element_type=F32,
-            )
-            for n, c in units:
-                spread[n // 4, pl.ds((n % 4) * 2 + w, owners, stride=8), :] = picked[
-                    :, c * BLK : (c + 1) * BLK
-                ]
+    for w in range(2):
+        picked = jnp.dot(pick_ref[...], rows_ref[w], preferred_element_type=F32)
+        for n, (o, c) in enumerate(EARLY_UNITS + LATE_UNITS):
+            spread[n // 4, pl.ds((n % 4) * 2 + w, owners, stride=8), :] = picked[
+                o * owners : (o + 1) * owners, c * BLK : (c + 1) * BLK
+            ]
     for g in range(EARLY_GROUPS):
         early_ref[:, 0, g] = spread[g].reshape(owners, 8, BLK).astype(BF16)
     late_ref[:, 0] = spread[EARLY_GROUPS].reshape(owners, 8, BLK).astype(BF16)
@@ -81,10 +74,10 @@
     return jnp.dot(order, rows, preferred_element_type=F32)
 
 
-def row_energies(energy_ref, p, base):
+def row_energies(energy_ref, p, base, rows):
     parts = [
-        energy_ref[p, :, pl.ds(pl.multiple_of(base + i * BLK, BLK), BLK)].reshape(BLK, 1)
-        for i in range(VB // 2)
+        energy_ref[p, :, pl.ds(pl.multiple_of(base + i, BLK), BLK)].reshape(BLK, 1)
+        for i in range(0, rows, BLK)
     ]
     return jnp.concatenate(parts, axis=0)
 
@@ -100,96 +93,126 @@
     return jnp.where(live, -product / denominator, 0.0).astype(BF16)
 
 
+def unpacked(order, source):
+    pairs = source.shape[0] // 2
+    for g in range(0, EARLY_GROUPS, 2):
+        halves = [
+            sorted_rows(order, [source[s * pairs : (s + 1) * pairs, g + i] for i in range(2)])
+            for s in range(2)
+        ]
+        for i in range(2):
+            for j in range(4):
+                o, c = EARLY_UNITS[(g + i) * 4 + j]
+                yield o, c, jnp.concatenate(
+                    [x[j * HALF : (j + 1) * HALF, i * BLK : (i + 1) * BLK] for x in halves],
+                    axis=0,
+                ).astype(BF16)
+
+
 def middle_kernel(
     vir_ref, fit_ref, count_ref, occ_ref, aux_ref, early_ref,
     order_ref, own_ref, other_ref, energy_ref,
     out_ref, left1_ref,
-    blocks, first, second, left0,
+    blocks, first, second, left0, left1, sent,
 ):
     step = pl.program_id(0)
-    pairs = own_ref.shape[0] // 2
     half_blocks = VB // 2
     rows = half_blocks * BLK
     aux = aux_ref[0]
-    for h, source in enumerate((own_ref, other_ref)):
-        at = pl.multiple_of((h * OFB + step) * BLK, BLK)
-        for g in range(0, EARLY_GROUPS, 2):
-            halves = [
-                sorted_rows(
-                    order_ref[...],
-                    [source[s * pairs : (s + 1) * pairs, g + i] for i in range(2)],
+    copies = [
+        pltpu.make_async_copy(
+            left1.at[k], left1_ref.at[pl.ds(k * rows, rows)], sent.at[k]
+        )
+        for k in range(OCC_DEV)
+    ]
+
+    @pl.when(step < OFB)
+    def _():
+        for h, source in enumerate((own_ref, other_ref)):
+            at = pl.multiple_of((h * OFB + step) * BLK, BLK)
+            for o, c, block in unpacked(order_ref[...], source):
+                if o < 2:
+                    blocks[h, o * ODB + c, step] = block.T
+                elif o == 2:
+                    first[pl.ds(at, BLK), c * BLK : (c + 1) * BLK] = block
+                else:
+                    second[pl.ds(at, BLK), c * BLK : (c + 1) * BLK] = block
+
+    def multiply(m, k, left, right, turns):
+        p = k * PARTNERS + m
+        left[...] = jnp.zeros_like(left)
+        for h in range(2):
+
+            @pl.loop(0, count_ref[p, 1])
+            def _(f):
+                left_pos = fit_ref[h, p, 0, f]
+                at = pl.multiple_of((h * OFB + fit_ref[h, p, 1, f]) * BLK, BLK)
+                for v in range(half_blocks):
+                    c = vir_ref[p, 0, aux * half_blocks + v]
+                    left[v * BLK : (v + 1) * BLK, pl.ds(at, BLK)] = blocks[
+                        h, k * ODB + c, left_pos
+                    ]
+
+        if m == 1:
+            copies[k].start()
+        base = aux * rows
+        row_energy = row_energies(energy_ref, p, base, rows)
+        out_ref[...] = jnp.zeros_like(out_ref)
+        live_count = count_ref[p, 0]
+        live_turns = jnp.int32(0)
+        for i in range(turns):
+            leading = early_ref[p, i * 2] if m == 1 else i * 2
+            live_turns += (leading < live_count).astype(jnp.int32)
+
+        @pl.loop(0, jnp.where(aux * half_blocks < live_count, live_turns, 0))
+        def _(i):
+            at = [i * 2 + n for n in range(2)]
+            if m == 1:
+                at = [early_ref[p, n] for n in at]
+            columns = [pl.multiple_of(vir_ref[p, 1, v] * BLK, BLK) for v in at]
+            product = jnp.dot(
+                left[...],
+                jnp.concatenate([right[:, pl.ds(c, BLK)] for c in columns], axis=1),
+                preferred_element_type=F32,
+            )
+            for n, v in enumerate(at):
+                out_ref[0, :, pl.ds(pl.multiple_of(v * BLK, BLK), BLK)] = amplitudes(
+                    product[:, n * BLK : (n + 1) * BLK],
+                    v, p, count_ref, occ_ref, energy_ref, base, row_energy,
                 )
-                for s in range(2)
-            ]
-            for i in range(2):
-                for j in range(4):
-                    o, c = EARLY_UNITS[(g + i) * 4 + j]
-                    block = jnp.concatenate(
-                        [x[j * HALF : (j + 1) * HALF, i * BLK : (i + 1) * BLK] for x in halves],
-                        axis=0,
-                    ).astype(BF16)
-                    if o < 2:
-                        blocks[h, o * ODB + c, step] = block.T
-                    elif o == 2:
-                        first[pl.ds(at, BLK), c * BLK : (c + 1) * BLK] = block
-                    else:
-                        second[pl.ds(at, BLK), c * BLK : (c + 1) * BLK] = block
-
-    @pl.when(step == pl.num_programs(0) - 1)
-    def _():
-        for m, left in enumerate((left0, left1_ref)):
-            left[...] = jnp.zeros_like(left)
-            for k in range(OCC_DEV):
-                p = k * PARTNERS + m
-                for h in range(2):
-
-                    @pl.loop(0, count_ref[p, 1])
-                    def _(f, p=p, k=k, h=h, left=left):
-                        left_pos = fit_ref[h, p, 0, f]
-                        at = pl.multiple_of((h * OFB + fit_ref[h, p, 1, f]) * BLK, BLK)
-                        for v in range(half_blocks):
-                            c = vir_ref[p, 0, aux * half_blocks + v]
-                            where = slice(k * rows + v * BLK, k * rows + (v + 1) * BLK)
-                            left[where, pl.ds(at, BLK)] = blocks[h, k * ODB + c, left_pos]
-
-        for m, (left, right, turns) in enumerate(
-            ((left0, first, VB // 2), (left1_ref, second, early_ref.shape[1] // 2))
-        ):
-
-            @pl.loop(0, OCC_DEV * turns)
-            def _(i, m=m, left=left, right=right, turns=turns):
-                k = i // turns
-                p = k * PARTNERS + m
-                base = aux * rows
-                row_energy = row_energies(energy_ref, p, base)
-                at = [(i % turns) * 2 + n for n in range(2)]
-                if m == 1:
-                    at = [early_ref[p, n] for n in at]
-                columns = [pl.multiple_of(vir_ref[p, 1, v] * BLK, BLK) for v in at]
-                product = jnp.dot(
-                    left[pl.ds(pl.multiple_of(k * rows, rows), rows), :],
-                    jnp.concatenate([right[:, pl.ds(c, BLK)] for c in columns], axis=1),
-                    preferred_element_type=F32,
-                )
-                for n, v in enumerate(at):
-                    out_ref[p, :, pl.ds(pl.multiple_of(v * BLK, BLK), BLK)] = amplitudes(
-                        product[:, n * BLK : (n + 1) * BLK],
-                        v, p, count_ref, occ_ref, energy_ref, base, row_energy,
-                    )
+
+    for k in range(OCC_DEV):
+
+        @pl.when(step == OFB + k)
+        def _(k=k):
+            multiply(1, k, left1.at[k], second, early_ref.shape[1] // 2)
+
+        @pl.when(step == OFB + OCC_DEV + k)
+        def _(k=k):
+            multiply(0, k, left0, first, VB // 2)
+            if k == OCC_DEV - 1:
+                for copy in copies:
+                    copy.wait()
 
 
 def middle(scalars, order, own, other, energies):
-    pairs = own.shape[0]
+    pairs = other.shape[0]
     depth = 2 * OFB * BLK
     rows = VB // 2 * BLK
-    raw = pl.BlockSpec((pairs // OFB, EARLY_GROUPS, 8, BLK), lambda f, *_: (f, 0, 0, 0))
-    out = jax.ShapeDtypeStruct((OCC_DEV * PARTNERS, rows, VB * BLK), BF16)
-    left1 = jax.ShapeDtypeStruct((OCC_DEV * rows, depth), BF16)
+    raw = pl.BlockSpec(
+        (pairs // OFB, EARLY_GROUPS, 8, BLK),
+        lambda f, *_: (jnp.minimum(f, OFB - 1), 0, 0, 0),
+    )
+
+    def out_block(f, *_):
+        turn = jnp.maximum(f - OFB, 0)
+        return (lax.rem(turn, OCC_DEV) * PARTNERS + 1 - turn // OCC_DEV, 0, 0)
+
     return pl.pallas_call(
         middle_kernel,
         grid_spec=pltpu.PrefetchScalarGridSpec(
             num_scalar_prefetch=len(scalars),
-            grid=(OFB,),
+            grid=(OFB + OCC_DEV * PARTNERS,),
             in_specs=[
                 pl.BlockSpec(order.shape, lambda f, *_: (0, 0)),
                 raw,
@@ -197,18 +220,23 @@
                 pl.BlockSpec(energies.shape, lambda f, *_: (0, 0, 0)),
             ],
             out_specs=[
-                pl.BlockSpec(out.shape, lambda f, *_: (0, 0, 0)),
-                pl.BlockSpec(left1.shape, lambda f, *_: (0, 0)),
+                pl.BlockSpec((1, rows, VB * BLK), out_block),
+                pl.BlockSpec(memory_space=pl.ANY),
             ],
             scratch_shapes=[
                 pltpu.VMEM((2, OCC_DEV * ODB, OFB, BLK, BLK), BF16),
                 pltpu.VMEM((depth, ODB * BLK), BF16),
                 pltpu.VMEM((depth, EARLY * BLK), BF16),
-                pltpu.VMEM(left1.shape, BF16),
+                pltpu.VMEM((rows, depth), BF16),
+                pltpu.VMEM((OCC_DEV, rows, depth), BF16),
+                pltpu.SemaphoreType.DMA((OCC_DEV,)),
             ],
         ),
-        out_shape=[out, left1],
-        compiler_params=pltpu.CompilerParams(vmem_limit_bytes=VMEM_LIMIT),
+        out_shape=[
+            jax.ShapeDtypeStruct((OCC_DEV * PARTNERS, rows, VB * BLK), BF16),
+            jax.ShapeDtypeStruct((OCC_DEV * rows, depth), BF16),
+        ],
+        compiler_params=pltpu.CompilerParams(vmem_limit_bytes=60 * 1024 * 1024),
         name="middle",
     )(*scalars, order, own, other, energies)
 
@@ -240,20 +268,27 @@
 
     out_ref[...] = before_ref[...]
     base = aux_ref[0] * left_ref.shape[0]
-    row_energy = row_energies(energy_ref, p, base)
+    row_energy = row_energies(energy_ref, p, base, left_ref.shape[0])
+    live_count = count_ref[p, 0]
     for turn in range(LATE // 2):
-        at = [late_ref[p, turn * 2 + n] for n in range(2)]
-        columns = [pl.multiple_of((vir_ref[p, 1, v] - EARLY) * BLK, BLK) for v in at]
-        product = jnp.dot(
-            left_ref[...],
-            jnp.concatenate([right[:, pl.ds(c, BLK)] for c in columns], axis=1),
-            preferred_element_type=F32,
-        )
-        for n, v in enumerate(at):
-            out_ref[0, :, pl.ds(pl.multiple_of(v * BLK, BLK), BLK)] = amplitudes(
-                product[:, n * BLK : (n + 1) * BLK],
-                v, p, count_ref, occ_ref, energy_ref, base, row_energy,
+        leading = late_ref[p, turn * 2]
+
+        @pl.when((leading < live_count) & (aux_ref[0] * (VB // 2) < live_count))
+        def _(turn=turn):
+            at = [late_ref[p, turn * 2 + n] for n in range(2)]
+            columns = [
+                pl.multiple_of((vir_ref[p, 1, v] - EARLY) * BLK, BLK) for v in at
+            ]
+            product = jnp.dot(
+                left_ref[...],
+                jnp.concatenate([right[:, pl.ds(c, BLK)] for c in columns], axis=1),
+                preferred_element_type=F32,
             )
+            for n, v in enumerate(at):
+                out_ref[0, :, pl.ds(pl.multiple_of(v * BLK, BLK), BLK)] = amplitudes(
+                    product[:, n * BLK : (n + 1) * BLK],
+                    v, p, count_ref, occ_ref, energy_ref, base, row_energy,
+                )
 
 
 def late_products(scalars, order, left1, own, other, energies, before):
@@ -314,9 +349,11 @@
         upto = numbers[None, :] <= numbers[:, None]
         rank = jnp.sum(jnp.where(flags[:, None, :] & upto, 1, 0), axis=2)
         total = rank[:, -1:]
-        nth = jnp.minimum(jnp.arange(1, length + 1, dtype=jnp.int32), total)
+        index = jnp.arange(1, length + 1, dtype=jnp.int32)
+        nth = jnp.minimum(index, total)
         hit = flags[:, None, :] & (rank[:, None, :] == nth[:, :, None])
-        return jnp.sum(jnp.where(hit, numbers, 0), axis=2)
+        found = jnp.sum(jnp.where(hit, numbers, 0), axis=2)
+        return jnp.where(index <= total + total % 2, found, VB)
 
     early_at = listed(~is_late, EARLY + 1)
     late_at = listed(is_late, LATE)

time: 326 us -> 320 us (0.982)
  Pallas kernels: 50 us -> 37.3 us
    pallas_call x1, Pallas kernels: 33 us -> 22.3 us  [middle(): pl.pallas_call(middle_kernel, grid_spec=pltpu.PrefetchScalarGridSpec(num_...]
    unnamed x32 -> x31, local copies, waits for them, and re-layouts: 6.59 us -> 6.64 us
  transfers between devices with their start and end apart: 4 -> 4, of which waited for: 2 -> 3; matrix products, arithmetic and copies ran while one was open for 2% -> 2% of each run, Pallas kernels for 10% -> 7%
where the time goes in v3:
time: 320 us; the launch traced here: 319 us
  blocking collectives  246 us (77%)
  Pallas kernels  37.3 us (12%)
  starting transfers between devices  13.8 us (4%)
  local copies, waits for them, and re-layouts  8.69 us (3%)
  waiting for transfers between devices  8.62 us (3%)
  other arithmetic  4.24 us (1%)
    all_to_all x1, blocking collectives, per_device(): early = lax.all_to_all(early, 'occ', 0, 0, tiled=True)  246 us
    pallas_call x1, Pallas kernels, middle(): pl.pallas_call(middle_kernel, grid_spec=pltpu.PrefetchScalarGridSpec(num_...  22.3 us
    pallas_call x1, Pallas kernels, pack(): pl.pallas_call(pack_kernel, grid=(ROWP,), in_specs=[pl.BlockSpec((4 * own...  9.18 us
    ppermute x3, starting transfers between devices, swap(): return lax.ppermute(x, 'aux', [(0, 1), (1, 0)])  7.06 us
    all_to_all x1, starting transfers between devices, per_device(): late = lax.all_to_all(late, 'occ', 0, 0, tiled=True)  6.78 us
    unnamed x31, local copies, waits for them, and re-layouts  6.64 us
  transfers between devices with their start and end apart: 4, of which 3 were waited for; matrix products, arithmetic and copies ran while one was open for 2% of the time, Pallas kernels for 7%

profile of v3, /device:TPU:1, one launch (start us, length us, event | category | flops | bytes accessed | tf_op | source)
XLA Modules:
  0.0 318.5 jit_solution(4646180697979171035)
XLA Ops:
  0.0 0.8 reshape.161
  0.9 0.2 fusion.pick_ref
  1.1 2.7 copy-done.1
  3.7 9.2 %pack.1 = (bf16[128,5,8,8,128]{4,3,2,1,0:T(8,128)(2,1)S(1)}, bf16[128,5,8,128]{3,2,1,0:T(8,128)(2,1)}) custom-call(bf16[512,256]{1,0:T(8,128)(2,1)S(1)} %fusion.pick_ref, bf16[10,256,1152]{2,1,0:T(8,128)(2,1)S(1)} %bitcast.19), custom_call_target="tpu_custom_call" | custom-call | tf_op jit(solution)/shard_map/pack/pallas_call | solution.py:49
  13.0 245.7 %all_to_all.10 = bf16[128,5,8,8,128]{4,3,2,1,0:T(8,128)(2,1)} all-to-all(bf16[128,5,8,8,128]{4,3,2,1,0:T(8,128)(2,1)S(1)} %get-tuple-element.11), channel_id=1, replica_groups=mesh['occ'=128,'aux'=2] {'occ'}, dimensions={0} | all-to-all | bytes 20971520 | tf_op jit(solution)/shard_map/all_to_all | solution.py:339
  258.6 4.2 %collective-permute-start.1 = (bf16[640,8,8,128]{3,2,1,0:T(8,128)(2,1)}, bf16[640,8,8,128]{3,2,1,0:T(8,128)(2,1)}, u32[]{:S(2)}, u32[]{:S(2)}) collective-permute-start(bf16[640,8,8,128]{3,2,1,0:T(8,128)(2,1)} %bitcast.10.own_ref), channel_id=1, source_target_pairs={{0,1},{1,0},{2,3},{3,2},{4,5},{5,4},{6,7},{7,6},{8,9},{9,8},{10,11... | collective-permute-start | bytes 31457288 | tf_op jit(solution)/shard_map/ppermute | solution.py:330
  262.8 6.8 %all-to-all-start.1 = ((bf16[128,5,8,128]{3,2,1,0:T(8,128)(2,1)}), bf16[128,5,8,128]{3,2,1,0:T(8,128)(2,1)S(1)}, u32[]{:S(2)}, u32[]{:S(2)}) async-start(bf16[128,5,8,128]{3,2,1,0:T(8,128)(2,1)} %get-tuple-element.13), calls=%async_computation.1 | async-start | bytes 2621440 | tf_op jit(solution)/shard_map/all_to_all | solution.py:340
  269.6 0.6 collective-permute-start
  270.3 0.1 stack_reshape.3
  270.5 0.1 copy.34.vir_ref
  270.6 0.2 select_reduce_fusion
  270.9 0.2 fusion.7
  271.1 0.1 copy.27
  271.2 0.3 select_reduce_fusion.2
  271.5 0.1 copy.28
  271.6 0.2 fusion.8
  271.9 0.5 pad_maximum_fusion.occ_ref
  272.4 0.6 compare_select_fusion.1.early_ref
  273.0 0.8 fusion.1.order_ref
  273.7 0.7 copy.31.count_ref
  274.4 0.6 broadcast_in_dim.88.energy_ref
  275.0 3.5 %collective-permute-done = s32[4,2,8]{2,1,0:T(2,128)S(1)} collective-permute-done((s32[4,2,8]{2,1,0:T(2,128)S(1)}, s32[4,2,8]{2,1,0:T(2,128)S(1)}, u32[]{:S(2)}, u32[]{:S(2)}) %collective-permute-start) | collective-permute-done | bytes 288 | tf_op jit(solution)/shard_map/ppermute | solution.py:330
  278.6 0.6 pad_add_fusion.fit_ref
  279.2 22.3 %middle.1 = (bf16[4,512,1024]{2,1,0:T(8,128)(2,1)}, bf16[1024,2560]{1,0:T(8,128)(2,1)}) custom-call(s32[4,2,8]{2,1,0:T(2,128)} %copy-done.5, s32[2,4,2,8]{3,2,1,0:T(2,128)} %pad_add_fusion.fit_ref, s32[4,2]{1,0:T(4,128)} %copy.31.count_ref, f32[2,4]{1,0:T(2,128)} %pad_maximum_fusion.occ_ref, s32[1]{0:T(128)} %bitcast.1.aux_ref, ...), custom_call_target="tpu_custom_call" | custom-call | tf_op jit(solution)/shard_map/middle/pallas_call | solution.py:211
  301.5 3.0 all-to-all-done.1
  304.5 2.4 collective-permute-start.2
  306.8 0.2 fusion.4
  307.1 0.2 select_reduce_fusion.3
  307.4 2.1 collective-permute-done.2.other_ref
  309.5 2.5 copy-done.2
  312.0 0.7 copy-done.6
  312.7 5.9 %late.1 = bf16[4,512,1024]{2,1,0:T(8,128)(2,1)} custom-call(s32[4,2,8]{2,1,0:T(2,128)S(1)} %copy-done.6, s32[4,4]{1,0:T(4,128)S(1)} %compare_select_fusion.2.late_ref, s32[4,2]{1,0:T(4,128)S(1)} %copy-done.7, f32[2,4]{1,0:T(2,128)S(1)} %copy-done.8, s32[1]{0:T(128)} %bitcast.1.aux_ref, ...), custom_call_target="tpu_custom_call", output_to_operand_aliasing={{}: (10, {})} | custom-call | tf_op jit(solution)/shard_map/late/pallas_call | solution.py:298
  (43 shorter events, 0.8 us)
Async XLA Ops:
  0.0 270.4 %copy-start = (s32[512,2,8]{0,2,1:T(8,128)S(1)}, s32[512,2,8]{0,2,1:T(8,128)}, u32[]{:S(2)}) copy-start(s32[512,2,8]{0,2,1:T(8,128)} %param.9) | copy-start | bytes 98308
  1.1 2.7 copy-start.1
  12.9 256.6 %copy-start.10 = (s32[4,2,1,8]{3,2,1,0:T(1,128)S(1)}, s32[4,2,1,8]{3,2,1,0:T(1,128)}, u32[]{:S(2)}) copy-start(s32[4,2,1,8]{3,2,1,0:T(1,128)} %param.10) | copy-start | bytes 772
  12.9 257.2 %copy-start.11 = (s32[256]{0:T(256)S(1)}, s32[256]{0:T(256)}, u32[]{:S(2)}) copy-start(s32[256]{0:T(256)} %param.8) | copy-start | bytes 3076
  12.9 257.3 %copy-start.13 = (f32[256]{0:T(256)S(1)}, f32[256]{0:T(256)}, u32[]{:S(2)}) copy-start(f32[256]{0:T(256)} %param.13) | copy-start | bytes 3076
  12.9 260.8 %copy-start.12 = (s32[4,2]{0,1:T(2,128)S(1)}, s32[4,2]{0,1:T(2,128)}, u32[]{:S(2)}) copy-start(s32[4,2]{0,1:T(2,128)} %param.11) | copy-start | bytes 100
  12.9 261.5 %copy-start.9 = (f32[4,1024]{1,0:T(4,128)S(1)}, f32[4,1024]{1,0:T(4,128)}, u32[]{:S(2)}) copy-start(f32[4,1024]{1,0:T(4,128)} %param.12) | copy-start | bytes 49156
  258.6 20.5 %collective-permute-start.1 = (bf16[640,8,8,128]{3,2,1,0:T(8,128)(2,1)}, bf16[640,8,8,128]{3,2,1,0:T(8,128)(2,1)}, u32[]{:S(2)}, u32[]{:S(2)}) collective-permute-start(bf16[640,8,8,128]{3,2,1,0:T(8,128)(2,1)} %bitcast.10.own_ref), channel_id=1, source_target_pairs={{0,1},{1,0},{2,3},{3,2},{4,5},{5,4},{6,7},{7,6},{8,9},{9,8},{10,11... | collective-permute-start | bytes 31457288 | tf_op jit(solution)/shard_map/ppermute | solution.py:330
  262.8 41.7 %all-to-all-start.1 = ((bf16[128,5,8,128]{3,2,1,0:T(8,128)(2,1)}), bf16[128,5,8,128]{3,2,1,0:T(8,128)(2,1)S(1)}, u32[]{:S(2)}, u32[]{:S(2)}) async-start(bf16[128,5,8,128]{3,2,1,0:T(8,128)(2,1)} %get-tuple-element.13), calls=%async_computation.1 | async-start | bytes 2621440 | tf_op jit(solution)/shard_map/all_to_all | solution.py:340
  269.6 9.0 %collective-permute-start = (s32[4,2,8]{2,1,0:T(2,128)S(1)}, s32[4,2,8]{2,1,0:T(2,128)S(1)}, u32[]{:S(2)}, u32[]{:S(2)}) collective-permute-start(s32[4,2,8]{2,1,0:T(2,128)S(1)} %bitcast.24), channel_id=1, source_target_pairs={{0,1},{1,0},{2,3},{3,2},{4,5},{5,4},{6,7},{7,6},{8,9},{9,8},{10,11... | collective-permute-start | bytes 776 | tf_op jit(solution)/shard_map/ppermute | solution.py:330
  270.6 8.6 %copy-start.5 = (s32[4,2,8]{2,1,0:T(2,128)}, s32[4,2,8]{2,1,0:T(2,128)S(1)}, u32[]{:S(2)}) copy-start(s32[4,2,8]{2,1,0:T(2,128)S(1)} %copy.34.vir_ref) | copy-start | bytes 772
  279.2 30.3 %copy-start.3 = (bf16[256,256]{1,0:T(8,128)(2,1)S(1)}, bf16[256,256]{1,0:T(8,128)(2,1)}, u32[]{:S(2)}) copy-start(bf16[256,256]{1,0:T(8,128)(2,1)} %fusion.1.order_ref) | copy-start | bytes 393220
  279.2 30.3 %copy-start.4 = (f32[4,1,1024]{2,1,0:T(1,128)S(1)}, f32[4,1,1024]{2,1,0:T(1,128)}, u32[]{:S(2)}) copy-start(f32[4,1,1024]{2,1,0:T(1,128)} %broadcast_in_dim.88.energy_ref) | copy-start | bytes 49156
  279.2 30.3 %copy-start.7 = (s32[4,2]{1,0:T(4,128)S(1)}, s32[4,2]{1,0:T(4,128)}, u32[]{:S(2)}) copy-start(s32[4,2]{1,0:T(4,128)} %copy.31.count_ref) | copy-start | bytes 100
  279.2 30.3 %copy-start.8 = (f32[2,4]{1,0:T(2,128)S(1)}, f32[2,4]{1,0:T(2,128)}, u32[]{:S(2)}) copy-start(f32[2,4]{1,0:T(2,128)} %pad_maximum_fusion.occ_ref) | copy-start | bytes 100
  304.5 5.0 %collective-permute-start.2 = (bf16[640,8,128]{2,1,0:T(8,128)(2,1)S(1)}, bf16[640,8,128]{2,1,0:T(8,128)(2,1)S(1)}, u32[]{:S(2)}, u32[]{:S(2)}) collective-permute-start(bf16[640,8,128]{2,1,0:T(8,128)(2,1)S(1)} %bitcast.20), channel_id=1, source_target_pairs={{0,1},{1,0},{2,3},{3,2},{4,5},{5,4},{6,7},{7,6},{8,9},{9,8},{10,11... | collective-permute-start | bytes 3932168 | tf_op jit(solution)/shard_map/ppermute | solution.py:330
  309.5 2.5 copy-start.2
  312.0 0.7 copy-start.6

commit v4 on v3

--- a/solution.py
+++ b/solution.py
@@ -241,6 +241,31 @@
     )(*scalars, order, own, other, energies)
 
 
+def stage_kernel(from_ref, to_ref, done):
+    copies = [
+        pltpu.make_async_copy(from_ref.at[part], to_ref.at[part], done.at[n])
+        for n, part in enumerate(
+            pl.ds(n * from_ref.shape[0] // 4, from_ref.shape[0] // 4) for n in range(4)
+        )
+    ]
+    for copy in copies:
+        copy.start()
+    for copy in copies:
+        copy.wait()
+
+
+def stage(x):
+    return pl.pallas_call(
+        stage_kernel,
+        in_specs=[pl.BlockSpec(memory_space=pl.ANY)],
+        out_specs=pl.BlockSpec(memory_space=pl.ANY),
+        out_shape=jax.ShapeDtypeStruct(x.shape, x.dtype),
+        scratch_shapes=[pltpu.SemaphoreType.DMA((4,))],
+        compiler_params=pltpu.CompilerParams(vmem_limit_bytes=1024 * 1024),
+        name="stage",
+    )(x)
+
+
 def late_kernel(
     vir_ref, late_ref, count_ref, occ_ref, aux_ref,
     order_ref, left_ref, own_ref, other_ref, energy_ref, before_ref,
@@ -375,7 +400,7 @@
     late, out = lax.optimization_barrier((late, out))
     late = late.reshape(owners * ROWP, 8, BLK)
     scalars = (vir, late_at, block_counts, occ_pair, aux)
-    return late_products(scalars, order, left1, late, swap(late), energies, out)
+    return late_products(scalars, order, stage(left1), late, swap(late), energies, out)
 
 
 def solution(mesh):

time: 320 us -> 318 us (level)
  transfers between devices with their start and end apart: 4 -> 4, of which waited for: 3 -> 2; matrix products, arithmetic and copies ran while one was open for 2% -> 2% of each run, Pallas kernels for 7% -> 7%
where the time goes in v4:
time: 318 us; the launch traced here: 315 us
  blocking collectives  246 us (77%)
  Pallas kernels  35.6 us (11%)
  starting transfers between devices  13.8 us (4%)
  local copies, waits for them, and re-layouts  8.5 us (3%)
  waiting for transfers between devices  7.07 us (2%)
  other arithmetic  4.24 us (1%)
    all_to_all x1, blocking collectives, per_device(): early = lax.all_to_all(early, 'occ', 0, 0, tiled=True)  246 us
    pallas_call x1, Pallas kernels, middle(): pl.pallas_call(middle_kernel, grid_spec=pltpu.PrefetchScalarGridSpec(num_...  21.8 us
    pallas_call x1, Pallas kernels, pack(): pl.pallas_call(pack_kernel, grid=(ROWP,), in_specs=[pl.BlockSpec((4 * own...  9.18 us
    ppermute x3, starting transfers between devices, swap(): return lax.ppermute(x, 'aux', [(0, 1), (1, 0)])  7.06 us
    all_to_all x1, starting transfers between devices, per_device(): late = lax.all_to_all(late, 'occ', 0, 0, tiled=True)  6.78 us
    unnamed x31, local copies, waits for them, and re-layouts  6.45 us
  transfers between devices with their start and end apart: 4, of which 2 were waited for; matrix products, arithmetic and copies ran while one was open for 2% of the time, Pallas kernels for 7%

profile of v4, /device:TPU:1, one launch (start us, length us, event | category | flops | bytes accessed | tf_op | source)
XLA Modules:
  0.0 315.0 jit_solution(11375286658127324981)
XLA Ops:
  0.0 0.8 reshape.161
  0.9 0.2 fusion.pick_ref
  1.1 2.7 copy-done.1
  3.7 9.2 %pack.1 = (bf16[128,5,8,8,128]{4,3,2,1,0:T(8,128)(2,1)S(1)}, bf16[128,5,8,128]{3,2,1,0:T(8,128)(2,1)}) custom-call(bf16[512,256]{1,0:T(8,128)(2,1)S(1)} %fusion.pick_ref, bf16[10,256,1152]{2,1,0:T(8,128)(2,1)S(1)} %bitcast.19), custom_call_target="tpu_custom_call" | custom-call | tf_op jit(solution)/shard_map/pack/pallas_call | solution.py:49
  13.0 245.7 %all_to_all.10 = bf16[128,5,8,8,128]{4,3,2,1,0:T(8,128)(2,1)} all-to-all(bf16[128,5,8,8,128]{4,3,2,1,0:T(8,128)(2,1)S(1)} %get-tuple-element.11), channel_id=1, replica_groups=mesh['occ'=128,'aux'=2] {'occ'}, dimensions={0} | all-to-all | bytes 20971520 | tf_op jit(solution)/shard_map/all_to_all | solution.py:364
  258.6 4.2 %collective-permute-start.1 = (bf16[640,8,8,128]{3,2,1,0:T(8,128)(2,1)}, bf16[640,8,8,128]{3,2,1,0:T(8,128)(2,1)}, u32[]{:S(2)}, u32[]{:S(2)}) collective-permute-start(bf16[640,8,8,128]{3,2,1,0:T(8,128)(2,1)} %bitcast.10.own_ref), channel_id=1, source_target_pairs={{0,1},{1,0},{2,3},{3,2},{4,5},{5,4},{6,7},{7,6},{8,9},{9,8},{10,11... | collective-permute-start | bytes 31457288 | tf_op jit(solution)/shard_map/ppermute | solution.py:355
  262.8 6.8 %all-to-all-start.1 = ((bf16[128,5,8,128]{3,2,1,0:T(8,128)(2,1)}), bf16[128,5,8,128]{3,2,1,0:T(8,128)(2,1)S(1)}, u32[]{:S(2)}, u32[]{:S(2)}) async-start(bf16[128,5,8,128]{3,2,1,0:T(8,128)(2,1)} %get-tuple-element.13), calls=%async_computation.1 | async-start | bytes 2621440 | tf_op jit(solution)/shard_map/all_to_all | solution.py:365
  269.6 0.6 collective-permute-start
  270.3 0.1 stack_reshape.3
  270.5 0.1 copy.34.vir_ref
  270.6 0.2 select_reduce_fusion
  270.9 0.2 fusion.7
  271.1 0.1 copy.27
  271.2 0.3 select_reduce_fusion.2
  271.5 0.1 copy.28
  271.6 0.2 fusion.8
  271.9 0.5 pad_maximum_fusion.occ_ref
  272.4 0.6 compare_select_fusion.1.early_ref
  273.0 0.8 fusion.1.order_ref
  273.7 0.7 copy.31.count_ref
  274.4 0.6 broadcast_in_dim.88.energy_ref
  275.0 3.5 %collective-permute-done = s32[4,2,8]{2,1,0:T(2,128)S(1)} collective-permute-done((s32[4,2,8]{2,1,0:T(2,128)S(1)}, s32[4,2,8]{2,1,0:T(2,128)S(1)}, u32[]{:S(2)}, u32[]{:S(2)}) %collective-permute-start) | collective-permute-done | bytes 288 | tf_op jit(solution)/shard_map/ppermute | solution.py:355
  278.6 0.6 pad_add_fusion.fit_ref
  279.2 21.8 %middle.1 = (bf16[4,512,1024]{2,1,0:T(8,128)(2,1)}, bf16[1024,2560]{1,0:T(8,128)(2,1)}) custom-call(s32[4,2,8]{2,1,0:T(2,128)} %copy-done.5, s32[2,4,2,8]{3,2,1,0:T(2,128)} %pad_add_fusion.fit_ref, s32[4,2]{1,0:T(4,128)} %copy.31.count_ref, f32[2,4]{1,0:T(2,128)} %pad_maximum_fusion.occ_ref, s32[1]{0:T(128)} %bitcast.1.aux_ref, ...), custom_call_target="tpu_custom_call" | custom-call | tf_op jit(solution)/shard_map/middle/pallas_call | solution.py:211
  300.9 3.5 %all-to-all-done.1 = bf16[128,5,8,128]{3,2,1,0:T(8,128)(2,1)S(1)} async-done(((bf16[128,5,8,128]{3,2,1,0:T(8,128)(2,1)}), bf16[128,5,8,128]{3,2,1,0:T(8,128)(2,1)S(1)}, u32[]{:S(2)}, u32[]{:S(2)}) %all-to-all-start.1) | async-done | bytes 1310752 | tf_op jit(solution)/shard_map/all_to_all | solution.py:365
  304.5 2.4 collective-permute-start.2
  306.8 0.2 fusion.4
  307.1 0.2 select_reduce_fusion.3
  307.4 2.5 copy-done.2
  309.9 0.4 stage.1.left_ref
  310.3 0.5 copy-done.3
  310.8 4.2 %late.1 = bf16[4,512,1024]{2,1,0:T(8,128)(2,1)} custom-call(s32[4,2,8]{2,1,0:T(2,128)S(1)} %copy-done.6, s32[4,4]{1,0:T(4,128)S(1)} %compare_select_fusion.2.late_ref, s32[4,2]{1,0:T(4,128)S(1)} %copy-done.7, f32[2,4]{1,0:T(2,128)S(1)} %copy-done.8, s32[1]{0:T(128)} %bitcast.1.aux_ref, ...), custom_call_target="tpu_custom_call", output_to_operand_aliasing={{}: (10, {})} | custom-call | tf_op jit(solution)/shard_map/late/pallas_call | solution.py:323
  (44 shorter events, 0.8 us)
Async XLA Ops:
  0.0 270.4 %copy-start = (s32[512,2,8]{0,2,1:T(8,128)S(1)}, s32[512,2,8]{0,2,1:T(8,128)}, u32[]{:S(2)}) copy-start(s32[512,2,8]{0,2,1:T(8,128)} %param.9) | copy-start | bytes 98308
  1.1 2.7 copy-start.1
  12.9 256.6 %copy-start.10 = (s32[4,2,1,8]{3,2,1,0:T(1,128)S(1)}, s32[4,2,1,8]{3,2,1,0:T(1,128)}, u32[]{:S(2)}) copy-start(s32[4,2,1,8]{3,2,1,0:T(1,128)} %param.10) | copy-start | bytes 772
  12.9 257.2 %copy-start.11 = (s32[256]{0:T(256)S(1)}, s32[256]{0:T(256)}, u32[]{:S(2)}) copy-start(s32[256]{0:T(256)} %param.8) | copy-start | bytes 3076
  12.9 257.3 %copy-start.13 = (f32[256]{0:T(256)S(1)}, f32[256]{0:T(256)}, u32[]{:S(2)}) copy-start(f32[256]{0:T(256)} %param.13) | copy-start | bytes 3076
  12.9 260.8 %copy-start.12 = (s32[4,2]{0,1:T(2,128)S(1)}, s32[4,2]{0,1:T(2,128)}, u32[]{:S(2)}) copy-start(s32[4,2]{0,1:T(2,128)} %param.11) | copy-start | bytes 100
  12.9 261.5 %copy-start.9 = (f32[4,1024]{1,0:T(4,128)S(1)}, f32[4,1024]{1,0:T(4,128)}, u32[]{:S(2)}) copy-start(f32[4,1024]{1,0:T(4,128)} %param.12) | copy-start | bytes 49156
  258.6 20.5 %collective-permute-start.1 = (bf16[640,8,8,128]{3,2,1,0:T(8,128)(2,1)}, bf16[640,8,8,128]{3,2,1,0:T(8,128)(2,1)}, u32[]{:S(2)}, u32[]{:S(2)}) collective-permute-start(bf16[640,8,8,128]{3,2,1,0:T(8,128)(2,1)} %bitcast.10.own_ref), channel_id=1, source_target_pairs={{0,1},{1,0},{2,3},{3,2},{4,5},{5,4},{6,7},{7,6},{8,9},{9,8},{10,11... | collective-permute-start | bytes 31457288 | tf_op jit(solution)/shard_map/ppermute | solution.py:355
  262.8 41.7 %all-to-all-start.1 = ((bf16[128,5,8,128]{3,2,1,0:T(8,128)(2,1)}), bf16[128,5,8,128]{3,2,1,0:T(8,128)(2,1)S(1)}, u32[]{:S(2)}, u32[]{:S(2)}) async-start(bf16[128,5,8,128]{3,2,1,0:T(8,128)(2,1)} %get-tuple-element.13), calls=%async_computation.1 | async-start | bytes 2621440 | tf_op jit(solution)/shard_map/all_to_all | solution.py:365
  269.6 9.0 %collective-permute-start = (s32[4,2,8]{2,1,0:T(2,128)S(1)}, s32[4,2,8]{2,1,0:T(2,128)S(1)}, u32[]{:S(2)}, u32[]{:S(2)}) collective-permute-start(s32[4,2,8]{2,1,0:T(2,128)S(1)} %bitcast.24), channel_id=1, source_target_pairs={{0,1},{1,0},{2,3},{3,2},{4,5},{5,4},{6,7},{7,6},{8,9},{9,8},{10,11... | collective-permute-start | bytes 776 | tf_op jit(solution)/shard_map/ppermute | solution.py:355
  270.6 8.6 %copy-start.5 = (s32[4,2,8]{2,1,0:T(2,128)}, s32[4,2,8]{2,1,0:T(2,128)S(1)}, u32[]{:S(2)}) copy-start(s32[4,2,8]{2,1,0:T(2,128)S(1)} %copy.34.vir_ref) | copy-start | bytes 772
  304.5 5.8 %collective-permute-start.2 = (bf16[640,8,128]{2,1,0:T(8,128)(2,1)S(1)}, bf16[640,8,128]{2,1,0:T(8,128)(2,1)S(1)}, u32[]{:S(2)}, u32[]{:S(2)}) collective-permute-start(bf16[640,8,128]{2,1,0:T(8,128)(2,1)S(1)} %bitcast.20), channel_id=1, source_target_pairs={{0,1},{1,0},{2,3},{3,2},{4,5},{5,4},{6,7},{7,6},{8,9},{9,8},{10,11... | collective-permute-start | bytes 3932168 | tf_op jit(solution)/shard_map/ppermute | solution.py:355
  307.4 2.5 copy-start.2
  309.9 0.9 copy-start.3
  309.9 0.9 copy-start.4
  309.9 0.9 copy-start.6
  309.9 0.9 copy-start.7
  309.9 0.9 copy-start.8

commit v5 on v4

--- a/solution.py
+++ b/solution.py
@@ -269,7 +269,7 @@
 def late_kernel(
     vir_ref, late_ref, count_ref, occ_ref, aux_ref,
     order_ref, left_ref, own_ref, other_ref, energy_ref, before_ref,
-    out_ref, right,
+    out_ref, right, tiles, sent,
 ):
     k = pl.program_id(0)
     p = k * PARTNERS + 1
@@ -291,10 +291,25 @@
                             j * HALF : (j + 1) * HALF, i * BLK : (i + 1) * BLK
                         ]
 
-    out_ref[...] = before_ref[...]
     base = aux_ref[0] * left_ref.shape[0]
     row_energy = row_energies(energy_ref, p, base, left_ref.shape[0])
     live_count = count_ref[p, 0]
+
+    def each(kk, act):
+        q = kk * PARTNERS + 1
+        for n in range(LATE):
+            v = late_ref[q, n]
+            first = late_ref[q, n // 2 * 2]
+            new = (v != first) if n % 2 else True
+            live = (first < count_ref[q, 0]) & (aux_ref[0] * (VB // 2) < count_ref[q, 0])
+
+            @pl.when(live & new)
+            def _(n=n, v=v):
+                at = pl.multiple_of(v * BLK, BLK)
+                act(pltpu.make_async_copy(
+                    tiles.at[kk, n], out_ref.at[q, :, pl.ds(at, BLK)], sent.at[kk, n]
+                ))
+
     for turn in range(LATE // 2):
         leading = late_ref[p, turn * 2]
 
@@ -310,16 +325,23 @@
                 preferred_element_type=F32,
             )
             for n, v in enumerate(at):
-                out_ref[0, :, pl.ds(pl.multiple_of(v * BLK, BLK), BLK)] = amplitudes(
+                tiles[k, turn * 2 + n] = amplitudes(
                     product[:, n * BLK : (n + 1) * BLK],
                     v, p, count_ref, occ_ref, energy_ref, base, row_energy,
                 )
 
+    each(k, lambda copy: copy.start())
+
+    @pl.when(k == pl.num_programs(0) - 1)
+    def _():
+        for kk in range(OCC_DEV):
+            each(kk, lambda copy: copy.wait())
+
 
 def late_products(scalars, order, left1, own, other, energies, before):
     depth = left1.shape[1]
     rows = left1.shape[0] // OCC_DEV
-    out = pl.BlockSpec((1, rows, VB * BLK), lambda k, *_: (k * PARTNERS + 1, 0, 0))
+    out = pl.BlockSpec(memory_space=pl.ANY)
     return pl.pallas_call(
         late_kernel,
         grid_spec=pltpu.PrefetchScalarGridSpec(
@@ -334,7 +356,11 @@
                 out,
             ],
             out_specs=out,
-            scratch_shapes=[pltpu.VMEM((depth, LATE * BLK), BF16)],
+            scratch_shapes=[
+                pltpu.VMEM((depth, LATE * BLK), BF16),
+                pltpu.VMEM((OCC_DEV, LATE, rows, BLK), BF16),
+                pltpu.SemaphoreType.DMA((OCC_DEV, LATE)),
+            ],
         ),
         out_shape=jax.ShapeDtypeStruct(before.shape, BF16),
         input_output_aliases={len(scalars) + 5: 0},

time: 318 us -> 318 us (level)
  no operation moved by 1% of the time
where the time goes in v5:
time: 318 us; the launch traced here: 313 us
  blocking collectives  246 us (77%)
  Pallas kernels  33.8 us (11%)
  starting transfers between devices  13.8 us (4%)
  local copies, waits for them, and re-layouts  8.5 us (3%)
  waiting for transfers between devices  6.74 us (2%)
  other arithmetic  4.24 us (1%)
    all_to_all x1, blocking collectives, per_device(): early = lax.all_to_all(early, 'occ', 0, 0, tiled=True)  246 us
    pallas_call x1, Pallas kernels, middle(): pl.pallas_call(middle_kernel, grid_spec=pltpu.PrefetchScalarGridSpec(num_...  22.1 us
    pallas_call x1, Pallas kernels, pack(): pl.pallas_call(pack_kernel, grid=(ROWP,), in_specs=[pl.BlockSpec((4 * own...  9.18 us
    ppermute x3, starting transfers between devices, swap(): return lax.ppermute(x, 'aux', [(0, 1), (1, 0)])  7.06 us
    all_to_all x1, starting transfers between devices, per_device(): late = lax.all_to_all(late, 'occ', 0, 0, tiled=True)  6.78 us
    unnamed x31, local copies, waits for them, and re-layouts  6.45 us
  transfers between devices with their start and end apart: 4, of which 2 were waited for; matrix products, arithmetic and copies ran while one was open for 2% of the time, Pallas kernels for 7%

profile of v5, /device:TPU:1, one launch (start us, length us, event | category | flops | bytes accessed | tf_op | source)
XLA Modules:
  0.0 313.0 jit_solution(3292146797804291699)
XLA Ops:
  0.0 0.8 reshape.161
  0.9 0.2 fusion.pick_ref
  1.1 2.7 copy-done.1
  3.7 9.2 %pack.1 = (bf16[128,5,8,8,128]{4,3,2,1,0:T(8,128)(2,1)S(1)}, bf16[128,5,8,128]{3,2,1,0:T(8,128)(2,1)}) custom-call(bf16[512,256]{1,0:T(8,128)(2,1)S(1)} %fusion.pick_ref, bf16[10,256,1152]{2,1,0:T(8,128)(2,1)S(1)} %bitcast.19), custom_call_target="tpu_custom_call" | custom-call | tf_op jit(solution)/shard_map/pack/pallas_call | solution.py:49
  13.0 245.7 %all_to_all.10 = bf16[128,5,8,8,128]{4,3,2,1,0:T(8,128)(2,1)} all-to-all(bf16[128,5,8,8,128]{4,3,2,1,0:T(8,128)(2,1)S(1)} %get-tuple-element.11), channel_id=1, replica_groups=mesh['occ'=128,'aux'=2] {'occ'}, dimensions={0} | all-to-all | bytes 20971520 | tf_op jit(solution)/shard_map/all_to_all | solution.py:390
  258.6 4.2 %collective-permute-start.1 = (bf16[640,8,8,128]{3,2,1,0:T(8,128)(2,1)}, bf16[640,8,8,128]{3,2,1,0:T(8,128)(2,1)}, u32[]{:S(2)}, u32[]{:S(2)}) collective-permute-start(bf16[640,8,8,128]{3,2,1,0:T(8,128)(2,1)} %bitcast.10.own_ref), channel_id=1, source_target_pairs={{0,1},{1,0},{2,3},{3,2},{4,5},{5,4},{6,7},{7,6},{8,9},{9,8},{10,11... | collective-permute-start | bytes 31457288 | tf_op jit(solution)/shard_map/ppermute | solution.py:381
  262.8 6.8 %all-to-all-start.1 = ((bf16[128,5,8,128]{3,2,1,0:T(8,128)(2,1)}), bf16[128,5,8,128]{3,2,1,0:T(8,128)(2,1)S(1)}, u32[]{:S(2)}, u32[]{:S(2)}) async-start(bf16[128,5,8,128]{3,2,1,0:T(8,128)(2,1)} %get-tuple-element.13), calls=%async_computation.1 | async-start | bytes 2621440 | tf_op jit(solution)/shard_map/all_to_all | solution.py:391
  269.6 0.6 collective-permute-start
  270.3 0.1 stack_reshape.3
  270.5 0.1 copy.34.vir_ref
  270.6 0.2 select_reduce_fusion
  270.9 0.2 fusion.7
  271.1 0.1 copy.27
  271.2 0.3 select_reduce_fusion.2
  271.5 0.1 copy.28
  271.6 0.2 fusion.8
  271.9 0.5 pad_maximum_fusion.occ_ref
  272.4 0.6 compare_select_fusion.1.early_ref
  273.0 0.8 fusion.1.order_ref
  273.7 0.7 copy.31.count_ref
  274.4 0.6 broadcast_in_dim.88.energy_ref
  275.0 3.5 %collective-permute-done = s32[4,2,8]{2,1,0:T(2,128)S(1)} collective-permute-done((s32[4,2,8]{2,1,0:T(2,128)S(1)}, s32[4,2,8]{2,1,0:T(2,128)S(1)}, u32[]{:S(2)}, u32[]{:S(2)}) %collective-permute-start) | collective-permute-done | bytes 288 | tf_op jit(solution)/shard_map/ppermute | solution.py:381
  278.6 0.6 pad_add_fusion.fit_ref
  279.2 22.1 %middle.1 = (bf16[4,512,1024]{2,1,0:T(8,128)(2,1)}, bf16[1024,2560]{1,0:T(8,128)(2,1)}) custom-call(s32[4,2,8]{2,1,0:T(2,128)} %copy-done.5, s32[2,4,2,8]{3,2,1,0:T(2,128)} %pad_add_fusion.fit_ref, s32[4,2]{1,0:T(4,128)} %copy.31.count_ref, f32[2,4]{1,0:T(2,128)} %pad_maximum_fusion.occ_ref, s32[1]{0:T(128)} %bitcast.1.aux_ref, ...), custom_call_target="tpu_custom_call" | custom-call | tf_op jit(solution)/shard_map/middle/pallas_call | solution.py:211
  301.3 3.2 %all-to-all-done.1 = bf16[128,5,8,128]{3,2,1,0:T(8,128)(2,1)S(1)} async-done(((bf16[128,5,8,128]{3,2,1,0:T(8,128)(2,1)}), bf16[128,5,8,128]{3,2,1,0:T(8,128)(2,1)S(1)}, u32[]{:S(2)}, u32[]{:S(2)}) %all-to-all-start.1) | async-done | bytes 1310752 | tf_op jit(solution)/shard_map/all_to_all | solution.py:391
  304.5 2.4 collective-permute-start.2
  306.8 0.2 fusion.4
  307.1 0.2 select_reduce_fusion.3
  307.4 2.5 copy-done.2
  309.9 0.4 stage.1.left_ref
  310.3 0.5 copy-done.3
  310.8 2.1 late.1
  (44 shorter events, 0.8 us)
Async XLA Ops:
  0.0 270.4 %copy-start = (s32[512,2,8]{0,2,1:T(8,128)S(1)}, s32[512,2,8]{0,2,1:T(8,128)}, u32[]{:S(2)}) copy-start(s32[512,2,8]{0,2,1:T(8,128)} %param.9) | copy-start | bytes 98308
  1.1 2.7 copy-start.1
  12.9 256.6 %copy-start.10 = (s32[4,2,1,8]{3,2,1,0:T(1,128)S(1)}, s32[4,2,1,8]{3,2,1,0:T(1,128)}, u32[]{:S(2)}) copy-start(s32[4,2,1,8]{3,2,1,0:T(1,128)} %param.10) | copy-start | bytes 772
  12.9 257.2 %copy-start.11 = (s32[256]{0:T(256)S(1)}, s32[256]{0:T(256)}, u32[]{:S(2)}) copy-start(s32[256]{0:T(256)} %param.8) | copy-start | bytes 3076
  12.9 257.3 %copy-start.13 = (f32[256]{0:T(256)S(1)}, f32[256]{0:T(256)}, u32[]{:S(2)}) copy-start(f32[256]{0:T(256)} %param.13) | copy-start | bytes 3076
  12.9 260.8 %copy-start.12 = (s32[4,2]{0,1:T(2,128)S(1)}, s32[4,2]{0,1:T(2,128)}, u32[]{:S(2)}) copy-start(s32[4,2]{0,1:T(2,128)} %param.11) | copy-start | bytes 100
  12.9 261.5 %copy-start.9 = (f32[4,1024]{1,0:T(4,128)S(1)}, f32[4,1024]{1,0:T(4,128)}, u32[]{:S(2)}) copy-start(f32[4,1024]{1,0:T(4,128)} %param.12) | copy-start | bytes 49156
  258.6 20.5 %collective-permute-start.1 = (bf16[640,8,8,128]{3,2,1,0:T(8,128)(2,1)}, bf16[640,8,8,128]{3,2,1,0:T(8,128)(2,1)}, u32[]{:S(2)}, u32[]{:S(2)}) collective-permute-start(bf16[640,8,8,128]{3,2,1,0:T(8,128)(2,1)} %bitcast.10.own_ref), channel_id=1, source_target_pairs={{0,1},{1,0},{2,3},{3,2},{4,5},{5,4},{6,7},{7,6},{8,9},{9,8},{10,11... | collective-permute-start | bytes 31457288 | tf_op jit(solution)/shard_map/ppermute | solution.py:381
  262.8 41.7 %all-to-all-start.1 = ((bf16[128,5,8,128]{3,2,1,0:T(8,128)(2,1)}), bf16[128,5,8,128]{3,2,1,0:T(8,128)(2,1)S(1)}, u32[]{:S(2)}, u32[]{:S(2)}) async-start(bf16[128,5,8,128]{3,2,1,0:T(8,128)(2,1)} %get-tuple-element.13), calls=%async_computation.1 | async-start | bytes 2621440 | tf_op jit(solution)/shard_map/all_to_all | solution.py:391
  269.6 9.0 %collective-permute-start = (s32[4,2,8]{2,1,0:T(2,128)S(1)}, s32[4,2,8]{2,1,0:T(2,128)S(1)}, u32[]{:S(2)}, u32[]{:S(2)}) collective-permute-start(s32[4,2,8]{2,1,0:T(2,128)S(1)} %bitcast.24), channel_id=1, source_target_pairs={{0,1},{1,0},{2,3},{3,2},{4,5},{5,4},{6,7},{7,6},{8,9},{9,8},{10,11... | collective-permute-start | bytes 776 | tf_op jit(solution)/shard_map/ppermute | solution.py:381
  270.6 8.6 %copy-start.5 = (s32[4,2,8]{2,1,0:T(2,128)}, s32[4,2,8]{2,1,0:T(2,128)S(1)}, u32[]{:S(2)}) copy-start(s32[4,2,8]{2,1,0:T(2,128)S(1)} %copy.34.vir_ref) | copy-start | bytes 772
  304.5 5.8 %collective-permute-start.2 = (bf16[640,8,128]{2,1,0:T(8,128)(2,1)S(1)}, bf16[640,8,128]{2,1,0:T(8,128)(2,1)S(1)}, u32[]{:S(2)}, u32[]{:S(2)}) collective-permute-start(bf16[640,8,128]{2,1,0:T(8,128)(2,1)S(1)} %bitcast.20), channel_id=1, source_target_pairs={{0,1},{1,0},{2,3},{3,2},{4,5},{5,4},{6,7},{7,6},{8,9},{9,8},{10,11... | collective-permute-start | bytes 3932168 | tf_op jit(solution)/shard_map/ppermute | solution.py:381
  307.4 2.5 copy-start.2
  309.9 0.9 copy-start.3
  309.9 0.9 copy-start.4
  309.9 0.9 copy-start.6
  309.9 0.9 copy-start.7
  309.9 0.9 copy-start.8
